TPU v7x, 256 devices: a whole 4x4x8 slice. The times are simulated.
256 devices in a mesh: ctx: 32 (over y, x, core), head: 8 (over z).
Axes of the slice: x: 4, y: 4, z: 8, core: 2. Of those that a mesh axis runs over, the one named last changes fastest.
Arguments:
- queries: bfloat16 [4096, 128, 576], P('ctx', 'head'), may hold values from -6 to 6
- out_grads: bfloat16 [4096, 128, 512], P('ctx', 'head'), may hold values from -6 to 6
- latent: bfloat16 [16384, 576], P('ctx'), may hold values from -6 to 6
- block_lists: int32 [64, 16], P('ctx'), may hold values from 0 to 255, as said below
- block_home: int32 [256], replicated, may hold values from 0 to 255, as said below
Outputs:
- query_grads: bfloat16 [4096, 128, 576], P('ctx', 'head')
- latent_grads: float32 [16384, 576], P('ctx')
Inputs may be any that keep to these rules, and one draw needn't show every extreme that they name: Block b is stored at rows block_home[b]*64 to block_home[b]*64 + 63 of latent; block_home is a permutation. `block_lists`: each row names distinct blocks. Among the 32 entries of the rows of one index of ctx, at most 2 name blocks whose block_home lies in one range o*8 to o*8 + 7, and some range is named exactly 2 times.
All inputs are finite; a program needn't handle non-finite values.
Results may differ from a plain program's by a relative error of at most 0.0058.
Values may be sent and summed in bfloat16 or wider, within the bound.
No kernel may reach another device: no remote copies, remote signals or barrier semaphores. Data moves between devices by JAX's collectives and lax.ppermute only.
A program may use at most 128 MiB of HBM per device.

v0:
```python
import functools

import jax
import jax.numpy as jnp
from jax import lax
from jax.experimental import pallas as pl
from jax.experimental.pallas import tpu as pltpu
from jax.sharding import PartitionSpec as P

BLK = 64
CAPACITY = 2
QUARTERS = 4
LOG2E = 1.4426950408889634
softmax_scale = 192.0 ** (-0.5)
VMEM_LIMIT = 56 * 1024 * 1024
ROWS_BY_ROWS = (((1,), (1,)), ((), ()))
COLS_BY_COLS = (((0,), (0,)), ((), ()))


def smem():
    return pl.BlockSpec(memory_space=pltpu.SMEM)


def vmem():
    return pl.BlockSpec(memory_space=pltpu.VMEM)


def plan_kernel(stored_blocks, lists_ref, home_ref, slot_ref, request_ref, entry_ref):
    groups, chosen = lists_ref.shape
    owners = request_ref.shape[0]
    for owner in range(owners):
        for copy in range(CAPACITY):
            request_ref[owner, 0, copy] = -1
            entry_ref[owner * CAPACITY + copy] = 0
    for group in range(groups):
        for at in range(chosen):
            entry = group * chosen + at
            stored = home_ref[lists_ref[group, at]]
            owner = stored // stored_blocks
            copy = jnp.where(request_ref[owner, 0, 0] >= 0, 1, 0)
            slot = owner * CAPACITY + copy
            slot_ref[entry] = slot
            request_ref[owner, 0, copy] = stored % stored_blocks
            entry_ref[slot] = entry


def plan(block_lists, block_home, ctx_count, stored_blocks):
    entries = block_lists.shape[0] * block_lists.shape[1]
    return pl.pallas_call(
        functools.partial(plan_kernel, stored_blocks),
        out_shape=(
            jax.ShapeDtypeStruct((entries,), jnp.int32),
            jax.ShapeDtypeStruct((ctx_count, 1, CAPACITY), jnp.int32),
            jax.ShapeDtypeStruct((ctx_count * CAPACITY,), jnp.int32),
        ),
        in_specs=[smem(), smem()],
        out_specs=(smem(), smem(), smem()),
        name="plan",
    )(block_lists, block_home)


def read_index(index_ref, at):
    if len(index_ref.shape) == 3:
        return index_ref[at // CAPACITY, 0, at % CAPACITY]
    return index_ref[at]


def take_kernel(index_ref, rows_ref, out_ref):
    for at in range(out_ref.shape[0]):
        out_ref[at] = rows_ref[jnp.maximum(read_index(index_ref, at), 0)]


def take(index, rows):
    return pl.pallas_call(
        take_kernel,
        out_shape=jax.ShapeDtypeStruct((index.size,) + rows.shape[1:], rows.dtype),
        in_specs=[smem(), vmem()],
        out_specs=vmem(),
        name="take",
    )(index, rows)


def pick_kernel(index_ref, rows_ref, out_ref):
    groups, subs, chosen = out_ref.shape[:3]
    for group in range(groups):
        for at in range(chosen):
            slot = index_ref[group * chosen + at]
            for sub in range(subs):
                out_ref[group, sub, at] = rows_ref[slot, sub]


def pick(index, rows, groups):
    chosen = index.shape[0] // groups
    shape = (groups, rows.shape[1], chosen) + rows.shape[2:]
    return pl.pallas_call(
        pick_kernel,
        out_shape=jax.ShapeDtypeStruct(shape, rows.dtype),
        in_specs=[smem(), vmem()],
        out_specs=vmem(),
        name="pick",
    )(index, rows)


def gather_sum_kernel(index_ref, rows_ref, out_ref, total):
    total[...] = jnp.zeros_like(total)
    stored = out_ref.shape[0]
    for at in range(rows_ref.shape[0]):
        index = read_index(index_ref, at)
        index = jnp.where(index < 0, stored, index)
        total[index] += rows_ref[at].astype(jnp.float32)
    out_ref[...] = total[:stored].astype(out_ref.dtype)


def gather_sum(index, rows, stored):
    return pl.pallas_call(
        gather_sum_kernel,
        out_shape=jax.ShapeDtypeStruct((stored,) + rows.shape[1:], jnp.bfloat16),
        in_specs=[smem(), vmem()],
        out_specs=vmem(),
        scratch_shapes=[pltpu.VMEM((stored + 1,) + rows.shape[1:], jnp.float32)],
        name="gather_sum",
    )(index, rows)


OFFSETS = ((0, 4), (1, -3), (-1, 3), (2, -2))


def group_kernel(value_width, me_ref, own_ref, *refs):
    key_refs = refs[:6]
    query_ref, grad_ref = refs[6:8]
    query_out = refs[8]
    part_refs = refs[9:17]
    keys, sums = refs[17:]
    step = pl.program_id(0)
    part = own_ref.shape[0]

    keys[:part, :] = own_ref[...]
    for group in range(2):

        @pl.when(step == group)
        def _():
            for at in range(3):
                keys[(at + 1) * part : (at + 2) * part, :] = key_refs[group * 3 + at][...]

    scores = lax.dot_general(
        keys[...], query_ref[...], ROWS_BY_ROWS, preferred_element_type=jnp.float32
    )
    factor = softmax_scale * LOG2E
    top = jnp.max(scores, axis=0, keepdims=True) * factor
    raised = jnp.exp2(scores * factor - top)
    weights = raised * (1.0 / jnp.sum(raised, axis=0, keepdims=True))
    half = weights.astype(jnp.bfloat16)
    weight_grad = lax.dot_general(
        keys[:, :value_width], grad_ref[...], ROWS_BY_ROWS, preferred_element_type=jnp.float32
    )
    delta = jnp.sum(half.astype(jnp.float32) * weight_grad, axis=0, keepdims=True)
    score_half = (weights * (weight_grad - delta)).astype(jnp.bfloat16)
    from_scores = (
        jnp.dot(score_half, query_ref[...], preferred_element_type=jnp.float32) * softmax_scale
    )
    from_values = jnp.dot(half, grad_ref[...], preferred_element_type=jnp.float32)
    sums[:, :value_width] = from_scores[:, :value_width] + from_values
    sums[:, value_width:] = from_scores[:, value_width:]
    query_out[...] = (
        lax.dot_general(
            keys[...], score_half, COLS_BY_COLS, preferred_element_type=jnp.float32
        )
        * softmax_scale
    ).astype(jnp.bfloat16)

    me = me_ref[0]
    half_part = part // 2
    for at in range(4):
        sub = ((me + OFFSETS[at][0] + 8) % 8) // 4
        for which in range(2):
            use = sub if which == 0 else 1 - sub
            start = pl.multiple_of(at * part + use * half_part, half_part)
            out = part_refs[at * 2 + which]
            out[...] = sums[pl.ds(start, half_part), :].astype(out.dtype)


def group_grads(me, own, key_parts, query_rows, grad_rows):
    groups, part, width = own.shape
    rows, value_width = grad_rows.shape[1:]
    key_count = QUARTERS * part
    by_group = lambda *shape: pl.BlockSpec((None,) + shape, lambda i: (i, 0, 0))
    whole = lambda *shape: pl.BlockSpec(shape, lambda i: (0, 0))
    out_shape = [jax.ShapeDtypeStruct((groups, width, rows), jnp.bfloat16)]
    out_specs = [by_group(width, rows)]
    for at in range(8):
        kind = jnp.float32 if at == 0 else jnp.bfloat16
        out_shape.append(jax.ShapeDtypeStruct((groups, part // 2, width), kind))
        out_specs.append(by_group(part // 2, width))
    flops = 2 * groups * rows * key_count * (3 * width + 2 * value_width)
    return pl.pallas_call(
        functools.partial(group_kernel, value_width),
        grid=(groups,),
        in_specs=[smem(), by_group(part, width)]
        + [whole(part, width)] * 6
        + [by_group(rows, width), by_group(rows, value_width)],
        out_specs=out_specs,
        out_shape=out_shape,
        scratch_shapes=[
            pltpu.VMEM((key_count, width), jnp.bfloat16),
            pltpu.VMEM((key_count, width), jnp.float32),
        ],
        compiler_params=pltpu.CompilerParams(vmem_limit_bytes=VMEM_LIMIT),
        cost_estimate=pl.CostEstimate(
            flops=flops, bytes_accessed=15_000_000, transcendentals=groups * rows * key_count
        ),
        name="group_grads",
    )(me, own, *key_parts, query_rows, grad_rows)


def shift(x, by):
    count = lax.axis_size("head")
    return lax.ppermute(x, "head", [(i, (i + by) % count) for i in range(count)])


def add(a, b):
    return (a.astype(jnp.float32) + b.astype(jnp.float32)).astype(jnp.bfloat16)


def ring_scatter(parts, group):
    if group == 0:
        right, left = shift(parts[4], 1), shift(parts[-3], -1)
        right = shift(add(parts[3], right), 1)
        left = shift(add(parts[-2], left), -1)
        right = shift(add(parts[2], right), 1)
        left = shift(add(parts[-1], left), -1)
        right = shift(add(parts[1], right), 1)
    else:
        right, left = shift(parts[3], 1), shift(parts[4], -1)
        right = shift(add(parts[2], right), 1)
        left = shift(add(parts[-3], left), -1)
        right = shift(add(parts[1], right), 1)
        left = shift(add(parts[-2], left), -1)
        left = shift(add(parts[-1], left), -1)
    total = parts[0] + right.astype(jnp.float32) + left.astype(jnp.float32)
    return total.astype(jnp.bfloat16)


def local(queries, out_grads, latent, block_lists, block_home):
    ctx_count = lax.axis_size("ctx")
    head_count = lax.axis_size("head")
    me = lax.axis_index("head")
    groups, chosen = block_lists.shape
    tokens, heads, width = queries.shape
    value_width = out_grads.shape[2]
    group_rows = tokens // groups
    stored_blocks = latent.shape[0] // BLK
    entries = groups * chosen
    share = BLK // head_count
    subs = head_count // QUARTERS
    rows = group_rows * heads

    slot_of, requests, entry_of = plan(block_lists, block_home, ctx_count, stored_blocks)
    requests_in = lax.all_to_all(requests, "ctx", split_axis=0, concat_axis=0, tiled=True)

    stored = latent.reshape(stored_blocks, QUARTERS, subs, share, width)
    mine = lax.dynamic_index_in_dim(stored, me % QUARTERS, 1, keepdims=False)
    query_rows = queries.reshape(groups, rows, width)
    grad_rows = out_grads.reshape(groups, rows, value_width)
    requests_in, mine, query_rows = lax.optimization_barrier((requests_in, mine, query_rows))

    arrived = lax.all_to_all(
        take(requests_in, mine), "ctx", split_axis=0, concat_axis=0, tiled=True
    )
    part = chosen * BLK // QUARTERS
    own = pick(slot_of, arrived, groups).reshape(groups, part, width)

    right0, right1 = shift(own[0], 1), shift(own[1], 1)
    left1, left0 = shift(own[1], -1), shift(own[0], -1)
    far0, far1 = shift(right0, 1), shift(left1, -1)

    key_parts = [left0, right0, far0, left1, right1, far1]
    me_ref = me.astype(jnp.int32).reshape(1)
    query_cols, *parts = group_grads(me_ref, own, key_parts, query_rows, grad_rows)
    sums = []
    for group in range(groups):
        by_offset = {}
        for at in range(4):
            for which in range(2):
                by_offset[OFFSETS[at][which]] = parts[at * 2 + which][group]
        sums.append(ring_scatter(by_offset, group))
    query_grads = query_cols.reshape(groups, width, group_rows, heads)
    query_grads = query_grads.transpose(0, 2, 3, 1).reshape(tokens, heads, width)

    summed = jnp.concatenate(sums, axis=0).reshape(entries, share, width)
    returned = lax.all_to_all(
        take(entry_of, summed), "ctx", split_axis=0, concat_axis=0, tiled=True
    )
    total = gather_sum(requests_in, returned, stored_blocks)

    minus1, minus2 = shift(total, 1), shift(total, 2)
    plus1, plus2 = shift(total, -1), shift(total, -2)
    minus3, plus3, minus4 = shift(minus2, 1), shift(plus2, -1), shift(minus2, 2)
    pieces = jnp.stack([total, plus1, plus2, plus3, minus4, minus3, minus2, minus1])
    pieces = jnp.roll(pieces, me, axis=0)
    pieces = pieces.reshape(subs, QUARTERS, stored_blocks, share, width)
    latent_grads = pieces.transpose(2, 1, 0, 3, 4).reshape(stored_blocks * BLK, width)
    return query_grads, latent_grads.astype(jnp.float32)


def solution(mesh):
    in_specs = (P("ctx", "head", None), P("ctx", "head", None), P("ctx", None), P("ctx", None), P())
    out_specs = (P("ctx", "head", None), P("ctx", None))
    return jax.shard_map(local, mesh=mesh, in_specs=in_specs, out_specs=out_specs, check_vma=False)
```

profile of v0, /device:TPU:2, one launch (start us, length us, event | category | flops | bytes accessed | tf_op | source)
XLA Modules:
  0.0 180.5 jit_solution(12088136004310794660)
XLA Ops:
  0.6 1.8 %plan.1 = (s32[32]{0:T(128)}, s32[32,1,2]{2,1,0:T(1,128)}, s32[64]{0:T(128)}) custom-call(s32[2,16]{1,0:T(2,128)} %lists_ref.1, s32[256]{0:T(256)} %home_ref.1), custom_call_target="tpu_custom_call" | custom-call | tf_op jit(solution)/shard_map/plan/pallas_call | solution.py:49
  2.5 7.6 %all-to-all-start = ((s32[32,1,2]{2,1,0:T(1,128)}), s32[32,1,2]{2,1,0:T(1,128)S(1)}, u32[]{:S(2)}, u32[]{:S(2)}) async-start(s32[32,1,2]{2,1,0:T(1,128)} %get-tuple-element.18), calls=%async_computation | async-start | bytes 32768 | tf_op jit(solution)/shard_map/all_to_all | solution.py:258
  10.1 1.4 copy.11
  12.2 4.9 %copy.12 = bf16[128,16,576]{2,1,0:T(8,128)(2,1)} copy(bf16[128,16,576]{0,2,1:T(8,128)(2,1)} %param.5) | data formatting | bytes 4718592 | tf_op args[0]
  17.6 2.1 %take.2 = bf16[64,2,8,576]{3,2,1,0:T(8,128)(2,1)} custom-call(s32[32,1,2]{2,1,0:T(1,128)} %copy-done.9, bf16[8,2,8,576]{3,2,1,0:T(8,128)(2,1)} %dynamic-slice_bitcast_fusion.rows_ref), custom_call_target="tpu_custom_call" | custom-call | tf_op jit(solution)/shard_map/take/pallas_call | solution.py:74
  19.8 26.4 %all_to_all.15.rows_ref = bf16[64,2,8,576]{3,2,1,0:T(8,128)(2,1)} all-to-all(bf16[64,2,8,576]{3,2,1,0:T(8,128)(2,1)} %take.2), channel_id=1, replica_groups=mesh['ctx'=32,'head'=8] {'ctx'}, dimensions={0} | all-to-all | bytes 2359296 | tf_op jit(solution)/shard_map/all_to_all | solution.py:266
  46.2 2.2 %pick.1 = bf16[2,2,16,8,576]{4,3,2,1,0:T(8,128)(2,1)} custom-call(s32[32]{0:T(128)} %get-tuple-element.17.index_ref, bf16[64,2,8,576]{3,2,1,0:T(8,128)(2,1)} %all_to_all.15.rows_ref), custom_call_target="tpu_custom_call" | custom-call | tf_op jit(solution)/shard_map/pick/pallas_call | solution.py:95
  48.4 1.1 fusion.14
  49.5 2.0 %collective-permute-start.1 = (bf16[256,576]{1,0:T(8,128)(2,1)S(1)}, bf16[256,576]{1,0:T(8,128)(2,1)S(1)}, u32[]{:S(2)}, u32[]{:S(2)}) collective-permute-start(bf16[256,576]{1,0:T(8,128)(2,1)S(1)} %bitcast.103), channel_id=1, source_target_pairs={{0,1},{1,2},{2,3},{3,4},{4,5},{5,6},{6,7},{7,0},{8,9},{9,10},{10,1... | collective-permute-start | bytes 884744 | tf_op jit(solution)/shard_map/ppermute | solution.py:217
  51.5 4.0 %collective-permute-start.3 = (bf16[256,576]{1,0:T(8,128)(2,1)S(1)}, bf16[256,576]{1,0:T(8,128)(2,1)S(1)}, u32[]{:S(2)}, u32[]{:S(2)}) collective-permute-start(bf16[256,576]{1,0:T(8,128)(2,1)S(1)} %bitcast.101), channel_id=1, source_target_pairs={{0,7},{1,0},{2,1},{3,2},{4,3},{5,4},{6,5},{7,6},{8,15},{9,8},{10,9... | collective-permute-start | bytes 884744 | tf_op jit(solution)/shard_map/ppermute | solution.py:217
  55.5 1.9 %collective-permute-start = (bf16[256,576]{1,0:T(8,128)(2,1)S(1)}, bf16[256,576]{1,0:T(8,128)(2,1)S(1)}, u32[]{:S(2)}, u32[]{:S(2)}) collective-permute-start(bf16[256,576]{1,0:T(8,128)(2,1)S(1)} %bitcast.104), channel_id=1, source_target_pairs={{0,7},{1,0},{2,1},{3,2},{4,3},{5,4},{6,5},{7,6},{8,15},{9,8},{10,9... | collective-permute-start | bytes 884744 | tf_op jit(solution)/shard_map/ppermute | solution.py:217
  57.6 6.4 %collective-permute-done.1.refs_1_ = bf16[256,576]{1,0:T(8,128)(2,1)S(1)} collective-permute-done((bf16[256,576]{1,0:T(8,128)(2,1)S(1)}, bf16[256,576]{1,0:T(8,128)(2,1)S(1)}, u32[]{:S(2)}, u32[]{:S(2)}) %collective-permute-start.1) | collective-permute-done | bytes 294944 | tf_op jit(solution)/shard_map/ppermute | solution.py:217
  64.0 3.2 %collective-permute-start.5 = (bf16[256,576]{1,0:T(8,128)(2,1)S(1)}, bf16[256,576]{1,0:T(8,128)(2,1)S(1)}, u32[]{:S(2)}, u32[]{:S(2)}) collective-permute-start(bf16[256,576]{1,0:T(8,128)(2,1)S(1)} %collective-permute-done.3.refs_3_), channel_id=1, source_target_pairs={{0,7},{1,0},{2,1},{3,2},{4,3},{5,4},{6,5},{7,6},{8,15},{9,8},{10,9... | collective-permute-start | bytes 884744 | tf_op jit(solution)/shard_map/ppermute | solution.py:217
  67.3 3.3 %collective-permute-done.refs_0_ = bf16[256,576]{1,0:T(8,128)(2,1)S(1)} collective-permute-done((bf16[256,576]{1,0:T(8,128)(2,1)S(1)}, bf16[256,576]{1,0:T(8,128)(2,1)S(1)}, u32[]{:S(2)}, u32[]{:S(2)}) %collective-permute-start) | collective-permute-done | bytes 294944 | tf_op jit(solution)/shard_map/ppermute | solution.py:217
  71.0 6.8 %collective-permute-done.2.refs_2_ = bf16[256,576]{1,0:T(8,128)(2,1)S(1)} collective-permute-done((bf16[256,576]{1,0:T(8,128)(2,1)S(1)}, bf16[256,576]{1,0:T(8,128)(2,1)S(1)}, u32[]{:S(2)}, u32[]{:S(2)}) %collective-permute-start.2) | collective-permute-done | bytes 294944 | tf_op jit(solution)/shard_map/ppermute | solution.py:217
  78.7 20.1 %group_grads.1 = (bf16[2,576,1024]{2,1,0:T(8,128)(2,1)}, f32[2,128,576]{2,1,0:T(8,128)}, bf16[2,128,576]{2,1,0:T(8,128)(2,1)}, bf16[2,128,576]{2,1,0:T(8,128)(2,...) custom-call(s32[1]{0:T(128)} %bitcast.me_ref, ...), custom_call_target="tpu_custom_call" | custom-call | flops 11542724608 | bytes 15000000 | tf_op jit(solution)/shard_map/group_grads/pallas_call | solution.py:195
  98.8 1.0 slice_bitcast_fusion.2
  99.8 3.0 %collective-permute-start.10 = (bf16[128,576]{1,0:T(8,128)(2,1)S(1)}, bf16[128,576]{1,0:T(8,128)(2,1)S(1)}, u32[]{:S(2)}, u32[]{:S(2)}) collective-permute-start(bf16[128,576]{1,0:T(8,128)(2,1)S(1)} %slice_bitcast_fusion.2), channel_id=1, source_target_pairs={{0,7},{1,0},{2,1},{3,2},{4,3},{5,4},{6,5},{7,6},{8,15},{9,8},{10,9... | collective-permute-start | bytes 442376 | tf_op jit(solution)/shard_map/ppermute | solution.py:217
  102.8 1.0 slice_bitcast_fusion.3
  103.9 0.9 slice_bitcast_fusion.1
  105.0 3.3 %collective-permute-start.16 = (bf16[128,576]{1,0:T(8,128)(2,1)S(1)}, bf16[128,576]{1,0:T(8,128)(2,1)S(1)}, u32[]{:S(2)}, u32[]{:S(2)}) collective-permute-start(bf16[128,576]{1,0:T(8,128)(2,1)S(1)} %get-tuple-element.43), channel_id=1, source_target_pairs={{0,7},{1,0},{2,1},{3,2},{4,3},{5,4},{6,5},{7,6},{8,15},{9,8},{10,9... | collective-permute-start | bytes 442376 | tf_op jit(solution)/shard_map/ppermute | solution.py:217
  108.3 4.0 %collective-permute-done.6 = bf16[128,576]{1,0:T(8,128)(2,1)S(1)} collective-permute-done((bf16[128,576]{1,0:T(8,128)(2,1)S(1)}, bf16[128,576]{1,0:T(8,128)(2,1)S(1)}, u32[]{:S(2)}, u32[]{:S(2)}) %collective-permute-start.6) | collective-permute-done | bytes 147488 | tf_op jit(solution)/shard_map/ppermute | solution.py:217
  112.5 3.3 %collective-permute-start.17 = (bf16[128,576]{1,0:T(8,128)(2,1)S(1)}, bf16[128,576]{1,0:T(8,128)(2,1)S(1)}, u32[]{:S(2)}, u32[]{:S(2)}) collective-permute-start(bf16[128,576]{1,0:T(8,128)(2,1)S(1)} %fusion), channel_id=1, source_target_pairs={{0,7},{1,0},{2,1},{3,2},{4,3},{5,4},{6,5},{7,6},{8,15},{9,8},{10,9... | collective-permute-start | bytes 442376 | tf_op jit(solution)/shard_map/ppermute | solution.py:217
  115.8 3.2 %collective-permute-done.7 = bf16[128,576]{1,0:T(8,128)(2,1)S(1)} collective-permute-done((bf16[128,576]{1,0:T(8,128)(2,1)S(1)}, bf16[128,576]{1,0:T(8,128)(2,1)S(1)}, u32[]{:S(2)}, u32[]{:S(2)}) %collective-permute-start.7) | collective-permute-done | bytes 147488 | tf_op jit(solution)/shard_map/ppermute | solution.py:217
  119.6 3.3 %collective-permute-start.11 = (bf16[128,576]{1,0:T(8,128)(2,1)S(1)}, bf16[128,576]{1,0:T(8,128)(2,1)S(1)}, u32[]{:S(2)}, u32[]{:S(2)}) collective-permute-start(bf16[128,576]{1,0:T(8,128)(2,1)S(1)} %get-tuple-element.46), channel_id=1, source_target_pairs={{0,7},{1,0},{2,1},{3,2},{4,3},{5,4},{6,5},{7,6},{8,15},{9,8},{10,9... | collective-permute-start | bytes 442376 | tf_op jit(solution)/shard_map/ppermute | solution.py:217
  122.9 1.9 %collective-permute-start.18 = (bf16[128,576]{1,0:T(8,128)(2,1)S(1)}, bf16[128,576]{1,0:T(8,128)(2,1)S(1)}, u32[]{:S(2)}, u32[]{:S(2)}) collective-permute-start(bf16[128,576]{1,0:T(8,128)(2,1)S(1)} %get-tuple-element.47), channel_id=1, source_target_pairs={{0,7},{1,0},{2,1},{3,2},{4,3},{5,4},{6,5},{7,6},{8,15},{9,8},{10,9... | collective-permute-start | bytes 442376 | tf_op jit(solution)/shard_map/ppermute | solution.py:217
  124.8 1.1 collective-permute-done.8
  125.9 2.1 %collective-permute-done.14 = bf16[128,576]{1,0:T(8,128)(2,1)S(1)} collective-permute-done((bf16[128,576]{1,0:T(8,128)(2,1)S(1)}, bf16[128,576]{1,0:T(8,128)(2,1)S(1)}, u32[]{:S(2)}, u32[]{:S(2)}) %collective-permute-start.14) | collective-permute-done | bytes 147488 | tf_op jit(solution)/shard_map/ppermute | solution.py:217
  129.1 3.3 %collective-permute-start.12 = (bf16[128,576]{1,0:T(8,128)(2,1)S(1)}, bf16[128,576]{1,0:T(8,128)(2,1)S(1)}, u32[]{:S(2)}, u32[]{:S(2)}) collective-permute-start(bf16[128,576]{1,0:T(8,128)(2,1)S(1)} %get-tuple-element.44), channel_id=1, source_target_pairs={{0,7},{1,0},{2,1},{3,2},{4,3},{5,4},{6,5},{7,6},{8,15},{9,8},{10,9... | collective-permute-start | bytes 442376 | tf_op jit(solution)/shard_map/ppermute | solution.py:217
  132.4 1.2 collective-permute-start.19
  133.6 1.1 collective-permute-done.9
  134.7 1.8 collective-permute-done.15
  136.4 1.3 collective-permute-done.19
  138.6 1.9 %take.3 = bf16[64,8,576]{2,1,0:T(8,128)(2,1)} custom-call(s32[64]{0:T(128)} %get-tuple-element.23.index_ref, bf16[32,8,576]{2,1,0:T(8,128)(2,1)} %maximum_bitcast_fusion.rows_ref), custom_call_target="tpu_custom_call" | custom-call | tf_op jit(solution)/shard_map/take/pallas_call | solution.py:74
  140.5 5.0 %all-to-all-start.2 = ((bf16[64,8,576]{2,1,0:T(8,128)(2,1)}), bf16[64,8,576]{2,1,0:T(8,128)(2,1)S(1)}, u32[]{:S(2)}, u32[]{:S(2)}) async-start(bf16[64,8,576]{2,1,0:T(8,128)(2,1)} %take.3), calls=%async_computation.2 | async-start | bytes 1310720 | tf_op jit(solution)/shard_map/all_to_all | solution.py:290
  145.4 3.1 %copy.13 = bf16[2,576,1024]{1,2,0:T(8,128)(2,1)S(1)} copy(bf16[2,576,1024]{2,1,0:T(8,128)(2,1)} %get-tuple-element.22) | data formatting | bytes 4718592 | tf_op jit(solution)/shard_map/group_grads/pallas_call | solution.py:195
  148.5 3.1 %copy.15 = bf16[128,16,576]{0,2,1:T(8,128)(2,1)} copy(bf16[128,16,576]{2,1,0:T(8,128)(2,1)S(1)} %bitcast.95) | data formatting | bytes 4718592
  151.6 5.8 %all-to-all-done.2.rows_ref = bf16[64,8,576]{2,1,0:T(8,128)(2,1)S(1)} async-done(((bf16[64,8,576]{2,1,0:T(8,128)(2,1)}), bf16[64,8,576]{2,1,0:T(8,128)(2,1)S(1)}, u32[]{:S(2)}, u32[]{:S(2)}) %all-to-all-start.2) | async-done | bytes 589856 | tf_op jit(solution)/shard_map/all_to_all | solution.py:290
  157.4 0.8 copy-done
  158.3 2.1 %gather_sum.1 = bf16[8,8,576]{2,1,0:T(8,128)(2,1)} custom-call(s32[32,1,2]{2,1,0:T(1,128)} %copy-done.9, bf16[64,8,576]{2,1,0:T(8,128)(2,1)} %copy-done), custom_call_target="tpu_custom_call" | custom-call | tf_op jit(solution)/shard_map/gather_sum/pallas_call | solution.py:115
  160.4 1.2 collective-permute-start.26
  161.6 3.5 %collective-permute-start.23 = (bf16[8,8,576]{2,1,0:T(8,128)(2,1)}, bf16[8,8,576]{2,1,0:T(8,128)(2,1)S(1)}, u32[]{:S(2)}, u32[]{:S(2)}) collective-permute-start(bf16[8,8,576]{2,1,0:T(8,128)(2,1)} %gather_sum.1), channel_id=1, source_target_pairs={{0,2},{1,3},{2,4},{3,5},{4,6},{5,7},{6,0},{7,1},{8,10},{9,11},{10,... | collective-permute-start | bytes 221192 | tf_op jit(solution)/shard_map/ppermute | solution.py:217
  166.6 0.9 bitcast_dynamic-update-slice_fusion.14
  167.5 3.7 %collective-permute-done.23 = bf16[8,8,576]{2,1,0:T(8,128)(2,1)S(1)} collective-permute-done((bf16[8,8,576]{2,1,0:T(8,128)(2,1)}, bf16[8,8,576]{2,1,0:T(8,128)(2,1)S(1)}, u32[]{:S(2)}, u32[]{:S(2)}) %collective-permute-start.23) | collective-permute-done | bytes 73760 | tf_op jit(solution)/shard_map/ppermute | solution.py:217
  171.3 1.0 collective-permute-start.24
  172.4 3.2 %collective-permute-start.22 = (bf16[8,8,576]{2,1,0:T(8,128)(2,1)S(1)}, bf16[8,8,576]{2,1,0:T(8,128)(2,1)S(1)}, u32[]{:S(2)}, u32[]{:S(2)}) collective-permute-start(bf16[8,8,576]{2,1,0:T(8,128)(2,1)S(1)} %collective-permute-done.21), channel_id=1, source_target_pairs={{0,7},{1,0},{2,1},{3,2},{4,3},{5,4},{6,5},{7,6},{8,15},{9,8},{10,9... | collective-permute-start | bytes 221192 | tf_op jit(solution)/shard_map/ppermute | solution.py:217
  175.7 3.0 %collective-permute-done.22 = bf16[8,8,576]{2,1,0:T(8,128)(2,1)S(1)} collective-permute-done((bf16[8,8,576]{2,1,0:T(8,128)(2,1)S(1)}, bf16[8,8,576]{2,1,0:T(8,128)(2,1)S(1)}, u32[]{:S(2)}, u32[]{:S(2)}) %collective-permute-start.22) | collective-permute-done | bytes 73760 | tf_op jit(solution)/shard_map/ppermute | solution.py:217
  179.1 1.4 copy.16
  (85 shorter events, 7.5 us)
Async XLA Ops:
  2.5 14.6 %all-to-all-start = ((s32[32,1,2]{2,1,0:T(1,128)}), s32[32,1,2]{2,1,0:T(1,128)S(1)}, u32[]{:S(2)}, u32[]{:S(2)}) async-start(s32[32,1,2]{2,1,0:T(1,128)} %get-tuple-element.18), calls=%async_computation | async-start | bytes 32768 | tf_op jit(solution)/shard_map/all_to_all | solution.py:258
  17.0 0.6 copy-start.9
  49.5 14.5 %collective-permute-start.1 = (bf16[256,576]{1,0:T(8,128)(2,1)S(1)}, bf16[256,576]{1,0:T(8,128)(2,1)S(1)}, u32[]{:S(2)}, u32[]{:S(2)}) collective-permute-start(bf16[256,576]{1,0:T(8,128)(2,1)S(1)} %bitcast.103), channel_id=1, source_target_pairs={{0,1},{1,2},{2,3},{3,4},{4,5},{5,6},{6,7},{7,0},{8,9},{9,10},{10,1... | collective-permute-start | bytes 884744 | tf_op jit(solution)/shard_map/ppermute | solution.py:217
  51.5 12.5 %collective-permute-start.3 = (bf16[256,576]{1,0:T(8,128)(2,1)S(1)}, bf16[256,576]{1,0:T(8,128)(2,1)S(1)}, u32[]{:S(2)}, u32[]{:S(2)}) collective-permute-start(bf16[256,576]{1,0:T(8,128)(2,1)S(1)} %bitcast.101), channel_id=1, source_target_pairs={{0,7},{1,0},{2,1},{3,2},{4,3},{5,4},{6,5},{7,6},{8,15},{9,8},{10,9... | collective-permute-start | bytes 884744 | tf_op jit(solution)/shard_map/ppermute | solution.py:217
  55.5 15.0 %collective-permute-start = (bf16[256,576]{1,0:T(8,128)(2,1)S(1)}, bf16[256,576]{1,0:T(8,128)(2,1)S(1)}, u32[]{:S(2)}, u32[]{:S(2)}) collective-permute-start(bf16[256,576]{1,0:T(8,128)(2,1)S(1)} %bitcast.104), channel_id=1, source_target_pairs={{0,7},{1,0},{2,1},{3,2},{4,3},{5,4},{6,5},{7,6},{8,15},{9,8},{10,9... | collective-permute-start | bytes 884744 | tf_op jit(solution)/shard_map/ppermute | solution.py:217
  57.5 13.6 %collective-permute-start.4 = (bf16[256,576]{1,0:T(8,128)(2,1)S(1)}, bf16[256,576]{1,0:T(8,128)(2,1)S(1)}, u32[]{:S(2)}, u32[]{:S(2)}) collective-permute-start(bf16[256,576]{1,0:T(8,128)(2,1)S(1)} %bitcast.102), channel_id=1, source_target_pairs={{0,1},{1,2},{2,3},{3,4},{4,5},{5,6},{6,7},{7,0},{8,9},{9,10},{10,1... | collective-permute-start | bytes 884744 | tf_op jit(solution)/shard_map/ppermute | solution.py:217
  64.0 13.8 %copy-start.10 = (bf16[256,576]{1,0:T(8,128)(2,1)}, bf16[256,576]{1,0:T(8,128)(2,1)S(1)}, u32[]{:S(2)}) copy-start(bf16[256,576]{1,0:T(8,128)(2,1)S(1)} %collective-permute-done.1.refs_1_) | copy-start | bytes 884740
  64.0 13.8 %collective-permute-start.2 = (bf16[256,576]{1,0:T(8,128)(2,1)S(1)}, bf16[256,576]{1,0:T(8,128)(2,1)S(1)}, u32[]{:S(2)}, u32[]{:S(2)}) collective-permute-start(bf16[256,576]{1,0:T(8,128)(2,1)S(1)} %collective-permute-done.1.refs_1_), channel_id=1, source_target_pairs={{0,1},{1,2},{2,3},{3,4},{4,5},{5,6},{6,7},{7,0},{8,9},{9,10},{10,1... | collective-permute-start | bytes 884744 | tf_op jit(solution)/shard_map/ppermute | solution.py:217
  64.0 13.8 %copy-start.11 = (bf16[256,576]{1,0:T(8,128)(2,1)}, bf16[256,576]{1,0:T(8,128)(2,1)S(1)}, u32[]{:S(2)}) copy-start(bf16[256,576]{1,0:T(8,128)(2,1)S(1)} %collective-permute-done.3.refs_3_) | copy-start | bytes 884740
  64.0 13.8 %collective-permute-start.5 = (bf16[256,576]{1,0:T(8,128)(2,1)S(1)}, bf16[256,576]{1,0:T(8,128)(2,1)S(1)}, u32[]{:S(2)}, u32[]{:S(2)}) collective-permute-start(bf16[256,576]{1,0:T(8,128)(2,1)S(1)} %collective-permute-done.3.refs_3_), channel_id=1, source_target_pairs={{0,7},{1,0},{2,1},{3,2},{4,3},{5,4},{6,5},{7,6},{8,15},{9,8},{10,9... | collective-permute-start | bytes 884744 | tf_op jit(solution)/shard_map/ppermute | solution.py:217
  70.6 7.3 %copy-start.12 = (bf16[256,576]{1,0:T(8,128)(2,1)}, bf16[256,576]{1,0:T(8,128)(2,1)S(1)}, u32[]{:S(2)}) copy-start(bf16[256,576]{1,0:T(8,128)(2,1)S(1)} %collective-permute-done.refs_0_) | copy-start | bytes 884740
  71.0 6.8 %copy-start.13 = (bf16[256,576]{1,0:T(8,128)(2,1)}, bf16[256,576]{1,0:T(8,128)(2,1)S(1)}, u32[]{:S(2)}) copy-start(bf16[256,576]{1,0:T(8,128)(2,1)S(1)} %collective-permute-done.4.refs_4_) | copy-start | bytes 884740
  77.8 0.7 copy-start.14
  77.8 0.8 copy-start.15
  98.8 13.5 %copy-start.4 = (bf16[2,128,576]{2,1,0:T(8,128)(2,1)S(1)}, bf16[2,128,576]{2,1,0:T(8,128)(2,1)}, u32[]{:S(2)}) copy-start(bf16[2,128,576]{2,1,0:T(8,128)(2,1)} %get-tuple-element.27) | copy-start | bytes 884740
  98.8 13.7 %copy-start.3 = (bf16[2,128,576]{2,1,0:T(8,128)(2,1)S(1)}, bf16[2,128,576]{2,1,0:T(8,128)(2,1)}, u32[]{:S(2)}) copy-start(bf16[2,128,576]{2,1,0:T(8,128)(2,1)} %get-tuple-element.31) | copy-start | bytes 884740
  98.8 20.2 %copy-start.8 = (bf16[2,128,576]{2,1,0:T(8,128)(2,1)S(1)}, bf16[2,128,576]{2,1,0:T(8,128)(2,1)}, u32[]{:S(2)}) copy-start(bf16[2,128,576]{2,1,0:T(8,128)(2,1)} %get-tuple-element.26) | copy-start | bytes 884740
  99.8 19.6 %collective-permute-start.10 = (bf16[128,576]{1,0:T(8,128)(2,1)S(1)}, bf16[128,576]{1,0:T(8,128)(2,1)S(1)}, u32[]{:S(2)}, u32[]{:S(2)}) collective-permute-start(bf16[128,576]{1,0:T(8,128)(2,1)S(1)} %slice_bitcast_fusion.2), channel_id=1, source_target_pairs={{0,7},{1,0},{2,1},{3,2},{4,3},{5,4},{6,5},{7,6},{8,15},{9,8},{10,9... | collective-permute-start | bytes 442376 | tf_op jit(solution)/shard_map/ppermute | solution.py:217
  103.8 15.6 %copy-start.7 = (bf16[2,128,576]{2,1,0:T(8,128)(2,1)S(1)}, bf16[2,128,576]{2,1,0:T(8,128)(2,1)}, u32[]{:S(2)}) copy-start(bf16[2,128,576]{2,1,0:T(8,128)(2,1)} %get-tuple-element.30) | copy-start | bytes 884740
  103.8 8.4 %collective-permute-start.6 = (bf16[128,576]{1,0:T(8,128)(2,1)S(1)}, bf16[128,576]{1,0:T(8,128)(2,1)S(1)}, u32[]{:S(2)}, u32[]{:S(2)}) collective-permute-start(bf16[128,576]{1,0:T(8,128)(2,1)S(1)} %get-tuple-element.42), channel_id=1, source_target_pairs={{0,1},{1,2},{2,3},{3,4},{4,5},{5,6},{6,7},{7,0},{8,9},{9,10},{10,1... | collective-permute-start | bytes 442376 | tf_op jit(solution)/shard_map/ppermute | solution.py:217
  104.9 10.9 %collective-permute-start.13 = (bf16[128,576]{1,0:T(8,128)(2,1)S(1)}, bf16[128,576]{1,0:T(8,128)(2,1)S(1)}, u32[]{:S(2)}, u32[]{:S(2)}) collective-permute-start(bf16[128,576]{1,0:T(8,128)(2,1)S(1)} %slice_bitcast_fusion.1), channel_id=1, source_target_pairs={{0,1},{1,2},{2,3},{3,4},{4,5},{5,6},{6,7},{7,0},{8,9},{9,10},{10,1... | collective-permute-start | bytes 442376 | tf_op jit(solution)/shard_map/ppermute | solution.py:217
  105.0 7.5 %collective-permute-start.16 = (bf16[128,576]{1,0:T(8,128)(2,1)S(1)}, bf16[128,576]{1,0:T(8,128)(2,1)S(1)}, u32[]{:S(2)}, u32[]{:S(2)}) collective-permute-start(bf16[128,576]{1,0:T(8,128)(2,1)S(1)} %get-tuple-element.43), channel_id=1, source_target_pairs={{0,7},{1,0},{2,1},{3,2},{4,3},{5,4},{6,5},{7,6},{8,15},{9,8},{10,9... | collective-permute-start | bytes 442376 | tf_op jit(solution)/shard_map/ppermute | solution.py:217
  112.3 15.6 %copy-start.6 = (bf16[2,128,576]{2,1,0:T(8,128)(2,1)S(1)}, bf16[2,128,576]{2,1,0:T(8,128)(2,1)}, u32[]{:S(2)}) copy-start(bf16[2,128,576]{2,1,0:T(8,128)(2,1)} %get-tuple-element.25) | copy-start | bytes 884740
  112.3 6.6 %collective-permute-start.7 = (bf16[128,576]{1,0:T(8,128)(2,1)S(1)}, bf16[128,576]{1,0:T(8,128)(2,1)S(1)}, u32[]{:S(2)}, u32[]{:S(2)}) collective-permute-start(bf16[128,576]{1,0:T(8,128)(2,1)S(1)} %fusion.7), channel_id=1, source_target_pairs={{0,1},{1,2},{2,3},{3,4},{4,5},{5,6},{6,7},{7,0},{8,9},{9,10},{10,1... | collective-permute-start | bytes 442376 | tf_op jit(solution)/shard_map/ppermute | solution.py:217
  112.5 7.0 %collective-permute-start.17 = (bf16[128,576]{1,0:T(8,128)(2,1)S(1)}, bf16[128,576]{1,0:T(8,128)(2,1)S(1)}, u32[]{:S(2)}, u32[]{:S(2)}) collective-permute-start(bf16[128,576]{1,0:T(8,128)(2,1)S(1)} %fusion), channel_id=1, source_target_pairs={{0,7},{1,0},{2,1},{3,2},{4,3},{5,4},{6,5},{7,6},{8,15},{9,8},{10,9... | collective-permute-start | bytes 442376 | tf_op jit(solution)/shard_map/ppermute | solution.py:217
  118.9 10.0 %copy-start.5 = (bf16[2,128,576]{2,1,0:T(8,128)(2,1)S(1)}, bf16[2,128,576]{2,1,0:T(8,128)(2,1)}, u32[]{:S(2)}) copy-start(bf16[2,128,576]{2,1,0:T(8,128)(2,1)} %get-tuple-element.29) | copy-start | bytes 884740
  119.0 6.8 %collective-permute-start.8 = (bf16[128,576]{1,0:T(8,128)(2,1)S(1)}, bf16[128,576]{1,0:T(8,128)(2,1)S(1)}, u32[]{:S(2)}, u32[]{:S(2)}) collective-permute-start(bf16[128,576]{1,0:T(8,128)(2,1)S(1)} %get-tuple-element.40), channel_id=1, source_target_pairs={{0,1},{1,2},{2,3},{3,4},{4,5},{5,6},{6,7},{7,0},{8,9},{9,10},{10,1... | collective-permute-start | bytes 442376 | tf_op jit(solution)/shard_map/ppermute | solution.py:217
  119.3 8.6 %collective-permute-start.14 = (bf16[128,576]{1,0:T(8,128)(2,1)S(1)}, bf16[128,576]{1,0:T(8,128)(2,1)S(1)}, u32[]{:S(2)}, u32[]{:S(2)}) collective-permute-start(bf16[128,576]{1,0:T(8,128)(2,1)S(1)} %get-tuple-element.41), channel_id=1, source_target_pairs={{0,1},{1,2},{2,3},{3,4},{4,5},{5,6},{6,7},{7,0},{8,9},{9,10},{10,1... | collective-permute-start | bytes 442376 | tf_op jit(solution)/shard_map/ppermute | solution.py:217
  119.5 18.2 %copy-start.2 = (f32[2,128,576]{2,1,0:T(8,128)S(1)}, f32[2,128,576]{2,1,0:T(8,128)}, u32[]{:S(2)}) copy-start(f32[2,128,576]{2,1,0:T(8,128)} %get-tuple-element.24) | copy-start | bytes 1769476
  119.6 9.3 %collective-permute-start.11 = (bf16[128,576]{1,0:T(8,128)(2,1)S(1)}, bf16[128,576]{1,0:T(8,128)(2,1)S(1)}, u32[]{:S(2)}, u32[]{:S(2)}) collective-permute-start(bf16[128,576]{1,0:T(8,128)(2,1)S(1)} %get-tuple-element.46), channel_id=1, source_target_pairs={{0,7},{1,0},{2,1},{3,2},{4,3},{5,4},{6,5},{7,6},{8,15},{9,8},{10,9... | collective-permute-start | bytes 442376 | tf_op jit(solution)/shard_map/ppermute | solution.py:217
  122.9 6.1 %collective-permute-start.18 = (bf16[128,576]{1,0:T(8,128)(2,1)S(1)}, bf16[128,576]{1,0:T(8,128)(2,1)S(1)}, u32[]{:S(2)}, u32[]{:S(2)}) collective-permute-start(bf16[128,576]{1,0:T(8,128)(2,1)S(1)} %get-tuple-element.47), channel_id=1, source_target_pairs={{0,7},{1,0},{2,1},{3,2},{4,3},{5,4},{6,5},{7,6},{8,15},{9,8},{10,9... | collective-permute-start | bytes 442376 | tf_op jit(solution)/shard_map/ppermute | solution.py:217
  128.0 6.6 %collective-permute-start.9 = (bf16[128,576]{1,0:T(8,128)(2,1)S(1)}, bf16[128,576]{1,0:T(8,128)(2,1)S(1)}, u32[]{:S(2)}, u32[]{:S(2)}) collective-permute-start(bf16[128,576]{1,0:T(8,128)(2,1)S(1)} %get-tuple-element.38), channel_id=1, source_target_pairs={{0,1},{1,2},{2,3},{3,4},{4,5},{5,6},{6,7},{7,0},{8,9},{9,10},{10,1... | collective-permute-start | bytes 442376 | tf_op jit(solution)/shard_map/ppermute | solution.py:217
  128.1 8.3 %collective-permute-start.15 = (bf16[128,576]{1,0:T(8,128)(2,1)S(1)}, bf16[128,576]{1,0:T(8,128)(2,1)S(1)}, u32[]{:S(2)}, u32[]{:S(2)}) collective-permute-start(bf16[128,576]{1,0:T(8,128)(2,1)S(1)} %get-tuple-element.39), channel_id=1, source_target_pairs={{0,1},{1,2},{2,3},{3,4},{4,5},{5,6},{6,7},{7,0},{8,9},{9,10},{10,1... | collective-permute-start | bytes 442376 | tf_op jit(solution)/shard_map/ppermute | solution.py:217
  129.1 7.3 %collective-permute-start.12 = (bf16[128,576]{1,0:T(8,128)(2,1)S(1)}, bf16[128,576]{1,0:T(8,128)(2,1)S(1)}, u32[]{:S(2)}, u32[]{:S(2)}) collective-permute-start(bf16[128,576]{1,0:T(8,128)(2,1)S(1)} %get-tuple-element.44), channel_id=1, source_target_pairs={{0,7},{1,0},{2,1},{3,2},{4,3},{5,4},{6,5},{7,6},{8,15},{9,8},{10,9... | collective-permute-start | bytes 442376 | tf_op jit(solution)/shard_map/ppermute | solution.py:217
  132.4 5.3 %collective-permute-start.19 = (bf16[128,576]{1,0:T(8,128)(2,1)S(1)}, bf16[128,576]{1,0:T(8,128)(2,1)S(1)}, u32[]{:S(2)}, u32[]{:S(2)}) collective-permute-start(bf16[128,576]{1,0:T(8,128)(2,1)S(1)} %get-tuple-element.45), channel_id=1, source_target_pairs={{0,7},{1,0},{2,1},{3,2},{4,3},{5,4},{6,5},{7,6},{8,15},{9,8},{10,9... | collective-permute-start | bytes 442376 | tf_op jit(solution)/shard_map/ppermute | solution.py:217
  140.5 17.0 %all-to-all-start.2 = ((bf16[64,8,576]{2,1,0:T(8,128)(2,1)}), bf16[64,8,576]{2,1,0:T(8,128)(2,1)S(1)}, u32[]{:S(2)}, u32[]{:S(2)}) async-start(bf16[64,8,576]{2,1,0:T(8,128)(2,1)} %take.3), calls=%async_computation.2 | async-start | bytes 1310720 | tf_op jit(solution)/shard_map/all_to_all | solution.py:290
  157.4 0.8 copy-start
  160.4 18.3 %copy-start.1 = (bf16[8,8,576]{2,1,0:T(8,128)(2,1)S(1)}, bf16[8,8,576]{2,1,0:T(8,128)(2,1)}, u32[]{:S(2)}) copy-start(bf16[8,8,576]{2,1,0:T(8,128)(2,1)} %gather_sum.1) | copy-start | bytes 221188
  160.4 18.3 %collective-permute-start.26 = (bf16[8,8,576]{2,1,0:T(8,128)(2,1)}, bf16[8,8,576]{2,1,0:T(8,128)(2,1)S(1)}, u32[]{:S(2)}, u32[]{:S(2)}) collective-permute-start(bf16[8,8,576]{2,1,0:T(8,128)(2,1)} %gather_sum.1), channel_id=1, source_target_pairs={{0,1},{1,2},{2,3},{3,4},{4,5},{5,6},{6,7},{7,0},{8,9},{9,10},{10,1... | collective-permute-start | bytes 221192 | tf_op jit(solution)/shard_map/ppermute | solution.py:217
  161.6 9.6 %collective-permute-start.23 = (bf16[8,8,576]{2,1,0:T(8,128)(2,1)}, bf16[8,8,576]{2,1,0:T(8,128)(2,1)S(1)}, u32[]{:S(2)}, u32[]{:S(2)}) collective-permute-start(bf16[8,8,576]{2,1,0:T(8,128)(2,1)} %gather_sum.1), channel_id=1, source_target_pairs={{0,2},{1,3},{2,4},{3,5},{4,6},{5,7},{6,0},{7,1},{8,10},{9,11},{10,... | collective-permute-start | bytes 221192 | tf_op jit(solution)/shard_map/ppermute | solution.py:217
  165.1 7.2 %collective-permute-start.21 = (bf16[8,8,576]{2,1,0:T(8,128)(2,1)}, bf16[8,8,576]{2,1,0:T(8,128)(2,1)S(1)}, u32[]{:S(2)}, u32[]{:S(2)}) collective-permute-start(bf16[8,8,576]{2,1,0:T(8,128)(2,1)} %gather_sum.1), channel_id=1, source_target_pairs={{0,6},{1,7},{2,0},{3,1},{4,2},{5,3},{6,4},{7,5},{8,14},{9,15},{10,... | collective-permute-start | bytes 221192 | tf_op jit(solution)/shard_map/ppermute | solution.py:217
  165.8 9.9 %collective-permute-start.20 = (bf16[8,8,576]{2,1,0:T(8,128)(2,1)}, bf16[8,8,576]{2,1,0:T(8,128)(2,1)S(1)}, u32[]{:S(2)}, u32[]{:S(2)}) collective-permute-start(bf16[8,8,576]{2,1,0:T(8,128)(2,1)} %gather_sum.1), channel_id=1, source_target_pairs={{0,7},{1,0},{2,1},{3,2},{4,3},{5,4},{6,5},{7,6},{8,15},{9,8},{10,9... | collective-permute-start | bytes 221192 | tf_op jit(solution)/shard_map/ppermute | solution.py:217
  171.2 7.5 %collective-permute-start.25 = (bf16[8,8,576]{2,1,0:T(8,128)(2,1)S(1)}, bf16[8,8,576]{2,1,0:T(8,128)(2,1)S(1)}, u32[]{:S(2)}, u32[]{:S(2)}) collective-permute-start(bf16[8,8,576]{2,1,0:T(8,128)(2,1)S(1)} %collective-permute-done.23), channel_id=1, source_target_pairs={{0,1},{1,2},{2,3},{3,4},{4,5},{5,6},{6,7},{7,0},{8,9},{9,10},{10,1... | collective-permute-start | bytes 221192 | tf_op jit(solution)/shard_map/ppermute | solution.py:217
  171.3 7.3 %collective-permute-start.24 = (bf16[8,8,576]{2,1,0:T(8,128)(2,1)S(1)}, bf16[8,8,576]{2,1,0:T(8,128)(2,1)S(1)}, u32[]{:S(2)}, u32[]{:S(2)}) collective-permute-start(bf16[8,8,576]{2,1,0:T(8,128)(2,1)S(1)} %collective-permute-done.23), channel_id=1, source_target_pairs={{0,2},{1,3},{2,4},{3,5},{4,6},{5,7},{6,0},{7,1},{8,10},{9,11},{10,... | collective-permute-start | bytes 221192 | tf_op jit(solution)/shard_map/ppermute | solution.py:217
  172.4 6.2 %collective-permute-start.22 = (bf16[8,8,576]{2,1,0:T(8,128)(2,1)S(1)}, bf16[8,8,576]{2,1,0:T(8,128)(2,1)S(1)}, u32[]{:S(2)}, u32[]{:S(2)}) collective-permute-start(bf16[8,8,576]{2,1,0:T(8,128)(2,1)S(1)} %collective-permute-done.21), channel_id=1, source_target_pairs={{0,7},{1,0},{2,1},{3,2},{4,3},{5,4},{6,5},{7,6},{8,15},{9,8},{10,9... | collective-permute-start | bytes 221192 | tf_op jit(solution)/shard_map/ppermute | solution.py:217
where the time goes:
time: 182 us; the launch traced here: 181 us
  starting transfers between devices  55.2 us (30%)
  waiting for transfers between devices  44 us (24%)
  Pallas kernels  30.3 us (17%)
  blocking collectives  26.4 us (15%)
  local copies, waits for them, and re-layouts  22.2 us (12%)
    ppermute x27, starting transfers between devices, shift(): lax.ppermute(x, 'head', [(i, (i + by) % count) for i in range(count)])  42.6 us
    ppermute x27, waiting for transfers between devices, shift(): lax.ppermute(x, 'head', [(i, (i + by) % count) for i in range(count)])  38.2 us
    all_to_all x1, blocking collectives, local(): lax.all_to_all(take(requests_in, mine), 'ctx', split_axis=0, concat_axis=...  26.4 us
    pallas_call x1, Pallas kernels, group_grads(): pl.pallas_call(functools.partial(group_kernel, value_width), grid=(groups...  20.1 us
    unnamed x51, local copies, waits for them, and re-layouts  14.1 us
    all_to_all x1, starting transfers between devices, local(): lax.all_to_all(requests, 'ctx', split_axis=0, concat_axis=0, tiled=True)  7.63 us
    all_to_all x1, waiting for transfers between devices, local(): lax.all_to_all(take(entry_of, summed), 'ctx', split_axis=0, concat_axis=0...  5.78 us
    all_to_all x1, starting transfers between devices, local(): lax.all_to_all(take(entry_of, summed), 'ctx', split_axis=0, concat_axis=0...  4.95 us
  transfers between devices with their start and end apart: 29, of which 15 were waited for; matrix products, arithmetic and copies ran while one was open for 9% of the time, Pallas kernels for 0%

commit v1 on v0

--- a/solution.py
+++ b/solution.py
@@ -80,25 +80,50 @@
     )(index, rows)
 
 
-def pick_kernel(index_ref, rows_ref, out_ref):
-    groups, subs, chosen = out_ref.shape[:3]
+def pick_kernel(index_ref, rows_ref, both_ref, *group_refs):
+    groups, subs, chosen = both_ref.shape[:3]
     for group in range(groups):
         for at in range(chosen):
             slot = index_ref[group * chosen + at]
             for sub in range(subs):
-                out_ref[group, sub, at] = rows_ref[slot, sub]
+                row = rows_ref[slot, sub]
+                both_ref[group, sub, at] = row
+                group_refs[group][sub, at] = row
 
 
 def pick(index, rows, groups):
     chosen = index.shape[0] // groups
-    shape = (groups, rows.shape[1], chosen) + rows.shape[2:]
+    shape = (rows.shape[1], chosen) + rows.shape[2:]
+    one = jax.ShapeDtypeStruct(shape, rows.dtype)
     return pl.pallas_call(
         pick_kernel,
-        out_shape=jax.ShapeDtypeStruct(shape, rows.dtype),
+        out_shape=[jax.ShapeDtypeStruct((groups,) + shape, rows.dtype)] + [one] * groups,
         in_specs=[smem(), vmem()],
-        out_specs=vmem(),
+        out_specs=[vmem()] * (groups + 1),
         name="pick",
     )(index, rows)
+
+
+def sum_take_kernel(index_ref, *refs):
+    term_refs, out_ref, total = refs[:-2], refs[-2], refs[-1]
+    value = term_refs[0][...].astype(jnp.float32)
+    for term in term_refs[1:]:
+        value = value + term[...].astype(jnp.float32)
+    total[...] = value.astype(total.dtype)
+    for at in range(out_ref.shape[0]):
+        out_ref[at] = total[index_ref[at]]
+
+
+def sum_take(index, terms):
+    kind = jnp.bfloat16
+    return pl.pallas_call(
+        sum_take_kernel,
+        out_shape=jax.ShapeDtypeStruct((index.shape[0],) + terms[0].shape[1:], kind),
+        in_specs=[smem()] + [vmem()] * len(terms),
+        out_specs=vmem(),
+        scratch_shapes=[pltpu.VMEM(terms[0].shape, kind)],
+        name="sum_take",
+    )(index, *terms)
 
 
 def gather_sum_kernel(index_ref, rows_ref, out_ref, total):
@@ -125,22 +150,22 @@
 OFFSETS = ((0, 4), (1, -3), (-1, 3), (2, -2))
 
 
-def group_kernel(value_width, me_ref, own_ref, *refs):
-    key_refs = refs[:6]
-    query_ref, grad_ref = refs[6:8]
-    query_out = refs[8]
-    part_refs = refs[9:17]
+def group_kernel(value_width, me_ref, *refs):
+    near_refs, far_refs = refs[:3], refs[3:5]
+    query_ref, grad_ref = refs[5:7]
+    query_out = refs[7]
+    part_refs = refs[8:17]
     keys, sums = refs[17:]
     step = pl.program_id(0)
-    part = own_ref.shape[0]
-
-    keys[:part, :] = own_ref[...]
+    part = near_refs[0].shape[0]
+
+    for at in range(3):
+        keys[at * part : (at + 1) * part, :] = near_refs[at][...]
     for group in range(2):
 
         @pl.when(step == group)
         def _():
-            for at in range(3):
-                keys[(at + 1) * part : (at + 2) * part, :] = key_refs[group * 3 + at][...]
+            keys[3 * part :, :] = far_refs[group][...]
 
     scores = lax.dot_general(
         keys[...], query_ref[...], ROWS_BY_ROWS, preferred_element_type=jnp.float32
@@ -175,28 +200,42 @@
         for which in range(2):
             use = sub if which == 0 else 1 - sub
             start = pl.multiple_of(at * part + use * half_part, half_part)
-            out = part_refs[at * 2 + which]
-            out[...] = sums[pl.ds(start, half_part), :].astype(out.dtype)
-
-
-def group_grads(me, own, key_parts, query_rows, grad_rows):
-    groups, part, width = own.shape
+            value = sums[pl.ds(start, half_part), :]
+            if OFFSETS[at][which] != 4:
+                out = part_refs[at * 2 + which]
+                out[...] = value.astype(out.dtype)
+                continue
+            for group in range(2):
+
+                @pl.when(step == group)
+                def _():
+                    out = part_refs[1 + 7 * group]
+                    out[...] = value.astype(out.dtype)
+
+
+def group_grads(me, near, far, query_rows, grad_rows):
+    groups, part, width = near[0].shape
     rows, value_width = grad_rows.shape[1:]
     key_count = QUARTERS * part
     by_group = lambda *shape: pl.BlockSpec((None,) + shape, lambda i: (i, 0, 0))
     whole = lambda *shape: pl.BlockSpec(shape, lambda i: (0, 0))
     out_shape = [jax.ShapeDtypeStruct((groups, width, rows), jnp.bfloat16)]
     out_specs = [by_group(width, rows)]
-    for at in range(8):
+    for at in range(9):
         kind = jnp.float32 if at == 0 else jnp.bfloat16
-        out_shape.append(jax.ShapeDtypeStruct((groups, part // 2, width), kind))
-        out_specs.append(by_group(part // 2, width))
+        if at in (1, 8):
+            out_shape.append(jax.ShapeDtypeStruct((part // 2, width), kind))
+            out_specs.append(whole(part // 2, width))
+        else:
+            out_shape.append(jax.ShapeDtypeStruct((groups, part // 2, width), kind))
+            out_specs.append(by_group(part // 2, width))
     flops = 2 * groups * rows * key_count * (3 * width + 2 * value_width)
     return pl.pallas_call(
         functools.partial(group_kernel, value_width),
         grid=(groups,),
-        in_specs=[smem(), by_group(part, width)]
-        + [whole(part, width)] * 6
+        in_specs=[smem()]
+        + [by_group(part, width)] * 3
+        + [whole(part, width)] * 2
         + [by_group(rows, width), by_group(rows, value_width)],
         out_specs=out_specs,
         out_shape=out_shape,
@@ -209,7 +248,7 @@
             flops=flops, bytes_accessed=15_000_000, transcendentals=groups * rows * key_count
         ),
         name="group_grads",
-    )(me, own, *key_parts, query_rows, grad_rows)
+    )(me, *near, *far, query_rows, grad_rows)
 
 
 def shift(x, by):
@@ -217,27 +256,21 @@
     return lax.ppermute(x, "head", [(i, (i + by) % count) for i in range(count)])
 
 
-def add(a, b):
-    return (a.astype(jnp.float32) + b.astype(jnp.float32)).astype(jnp.bfloat16)
-
-
-def ring_scatter(parts, group):
-    if group == 0:
-        right, left = shift(parts[4], 1), shift(parts[-3], -1)
-        right = shift(add(parts[3], right), 1)
-        left = shift(add(parts[-2], left), -1)
-        right = shift(add(parts[2], right), 1)
-        left = shift(add(parts[-1], left), -1)
-        right = shift(add(parts[1], right), 1)
-    else:
-        right, left = shift(parts[3], 1), shift(parts[4], -1)
-        right = shift(add(parts[2], right), 1)
-        left = shift(add(parts[-3], left), -1)
-        right = shift(add(parts[1], right), 1)
-        left = shift(add(parts[-2], left), -1)
-        left = shift(add(parts[-1], left), -1)
-    total = parts[0] + right.astype(jnp.float32) + left.astype(jnp.float32)
-    return total.astype(jnp.bfloat16)
+def add(*terms):
+    return sum(term.astype(jnp.float32) for term in terms).astype(jnp.bfloat16)
+
+
+def scatter_terms(outs):
+    plus, minus = {}, {}
+    own, far0, plus[1], minus[3], minus[1], plus[3], plus[2], minus[2], far1 = outs
+    from_left, from_right = shift(plus[3], 1), shift(minus[3], -1)
+    far_left, far_right = shift(far0, 2), shift(far1, -2)
+    near_left, near_right = shift(plus[1], 1), shift(minus[1], -1)
+    far_left = jnp.stack([far_left, jnp.zeros_like(far_left)])
+    far_right = jnp.stack([jnp.zeros_like(far_right), far_right])
+    two_left = shift(add(plus[2], from_left, far_left), 2)
+    two_right = shift(add(minus[2], from_right, far_right), -2)
+    return own, near_left, near_right, two_left, two_right
 
 
 def local(queries, out_grads, latent, block_lists, block_home):
@@ -267,28 +300,20 @@
         take(requests_in, mine), "ctx", split_axis=0, concat_axis=0, tiled=True
     )
     part = chosen * BLK // QUARTERS
-    own = pick(slot_of, arrived, groups).reshape(groups, part, width)
-
-    right0, right1 = shift(own[0], 1), shift(own[1], 1)
-    left1, left0 = shift(own[1], -1), shift(own[0], -1)
-    far0, far1 = shift(right0, 1), shift(left1, -1)
-
-    key_parts = [left0, right0, far0, left1, right1, far1]
+    own, own0, own1 = pick(slot_of, arrived, groups)
+    own = own.reshape(groups, part, width)
+    own0, own1 = own0.reshape(part, width), own1.reshape(part, width)
+
+    near = [own, shift(own, -1), shift(own, 1)]
+    far = [shift(own0, 2), shift(own1, -2)]
     me_ref = me.astype(jnp.int32).reshape(1)
-    query_cols, *parts = group_grads(me_ref, own, key_parts, query_rows, grad_rows)
-    sums = []
-    for group in range(groups):
-        by_offset = {}
-        for at in range(4):
-            for which in range(2):
-                by_offset[OFFSETS[at][which]] = parts[at * 2 + which][group]
-        sums.append(ring_scatter(by_offset, group))
+    query_cols, *outs = group_grads(me_ref, near, far, query_rows, grad_rows)
+    terms = [x.reshape(entries, share, width) for x in scatter_terms(outs)]
     query_grads = query_cols.reshape(groups, width, group_rows, heads)
     query_grads = query_grads.transpose(0, 2, 3, 1).reshape(tokens, heads, width)
 
-    summed = jnp.concatenate(sums, axis=0).reshape(entries, share, width)
     returned = lax.all_to_all(
-        take(entry_of, summed), "ctx", split_axis=0, concat_axis=0, tiled=True
+        sum_take(entry_of, terms), "ctx", split_axis=0, concat_axis=0, tiled=True
     )
     total = gather_sum(requests_in, returned, stored_blocks)
 

time: 182 us -> 194 us (1.066)
  waiting for transfers between devices: 44 us -> 57.7 us
  starting transfers between devices: 55.2 us -> 52.4 us
    ppermute x27 -> x19, waiting for transfers between devices: 38.2 us -> 52 us  [shift(): lax.ppermute(x, 'head', [(i, (i + by) % count) for i in range(count)])]
    pallas_call x1 -> x2, Pallas kernels: 2.22 us -> 5.19 us  [the longest x1 2.71 us: sum_take(): pl.pallas_call(sum_take_kernel, out_shape=jax.ShapeDtypeStruct((index.sha...]
    squeeze x3 -> x0, local copies, waits for them, and re-layouts: 2.97 us -> none  [local(): by_offset[OFFSETS[at][which]] = parts[at * 2 + which][group]]
    ppermute x27 -> x19, starting transfers between devices: 42.6 us -> 39.9 us  [shift(): lax.ppermute(x, 'head', [(i, (i + by) % count) for i in range(count)])]
    ppermute x0 -> x2, local copies, waits for them, and re-layouts: none -> 2.15 us  [shift(): lax.ppermute(x, 'head', [(i, (i + by) % count) for i in range(count)])]
    pallas_call x2 -> x1, Pallas kernels: 4.03 us -> 2.11 us  [take(): pl.pallas_call(take_kernel, out_shape=jax.ShapeDtypeStruct((index.size,)...]
    unnamed x51 -> x39, local copies, waits for them, and re-layouts: 14.1 us -> 14.8 us
  transfers between devices with their start and end apart: 29 -> 21, of which waited for: 15 -> 12; matrix products, arithmetic and copies ran while one was open for 9% -> 9% of each run, Pallas kernels for 0% -> 0%
where the time goes in v1:
time: 194 us; the launch traced here: 193 us
  waiting for transfers between devices  57.7 us (30%)
  starting transfers between devices  52.4 us (27%)
  Pallas kernels  32 us (16%)
  blocking collectives  26.4 us (14%)
  local copies, waits for them, and re-layouts  22.2 us (11%)
    ppermute x19, waiting for transfers between devices, shift(): lax.ppermute(x, 'head', [(i, (i + by) % count) for i in range(count)])  52 us
    ppermute x19, starting transfers between devices, shift(): lax.ppermute(x, 'head', [(i, (i + by) % count) for i in range(count)])  39.9 us
    all_to_all x1, blocking collectives, local(): lax.all_to_all(take(requests_in, mine), 'ctx', split_axis=0, concat_axis=...  26.4 us
    pallas_call x1, Pallas kernels, group_grads(): pl.pallas_call(functools.partial(group_kernel, value_width), grid=(groups...  20.8 us
    unnamed x39, local copies, waits for them, and re-layouts  14.8 us
    all_to_all x1, starting transfers between devices, local(): lax.all_to_all(requests, 'ctx', split_axis=0, concat_axis=0, tiled=True)  7.63 us
    all_to_all x1, waiting for transfers between devices, local(): lax.all_to_all(sum_take(entry_of, terms), 'ctx', split_axis=0, concat_axi...  5.69 us
    all_to_all x1, starting transfers between devices, local(): lax.all_to_all(sum_take(entry_of, terms), 'ctx', split_axis=0, concat_axi...  4.83 us
  transfers between devices with their start and end apart: 21, of which 12 were waited for; matrix products, arithmetic and copies ran while one was open for 9% of the time, Pallas kernels for 0%

profile of v1, /device:TPU:2, one launch (start us, length us, event | category | flops | bytes accessed | tf_op | source)
XLA Modules:
  0.0 192.8 jit_solution(2614659046124575605)
XLA Ops:
  0.6 1.8 plan.1
  2.5 7.6 %all-to-all-start = ((s32[32,1,2]{2,1,0:T(1,128)}), s32[32,1,2]{2,1,0:T(1,128)S(1)}, u32[]{:S(2)}, u32[]{:S(2)}) async-start(s32[32,1,2]{2,1,0:T(1,128)} %get-tuple-element.22), calls=%async_computation | async-start | bytes 32768 | tf_op jit(solution)/shard_map/all_to_all | solution.py:291
  10.1 1.4 copy.17
  12.2 4.9 %copy.18 = bf16[128,16,576]{2,1,0:T(8,128)(2,1)} copy(bf16[128,16,576]{0,2,1:T(8,128)(2,1)} %param.5) | data formatting | bytes 4718592 | tf_op args[0]
  17.7 2.1 %take.1 = bf16[64,2,8,576]{3,2,1,0:T(8,128)(2,1)} custom-call(s32[32,1,2]{2,1,0:T(1,128)} %copy-done.7, bf16[8,2,8,576]{3,2,1,0:T(8,128)(2,1)} %dynamic-slice_bitcast_fusion.rows_ref), custom_call_target="tpu_custom_call" | custom-call | tf_op jit(solution)/shard_map/take/pallas_call | solution.py:74
  19.8 26.4 %all_to_all.15.rows_ref = bf16[64,2,8,576]{3,2,1,0:T(8,128)(2,1)} all-to-all(bf16[64,2,8,576]{3,2,1,0:T(8,128)(2,1)} %take.1), channel_id=1, replica_groups=mesh['ctx'=32,'head'=8] {'ctx'}, dimensions={0} | all-to-all | bytes 2359296 | tf_op jit(solution)/shard_map/all_to_all | solution.py:299
  46.2 2.5 %pick.1 = (bf16[2,2,16,8,576]{4,3,2,1,0:T(8,128)(2,1)}, bf16[2,16,8,576]{3,2,1,0:T(8,128)(2,1)}, bf16[2,16,8,576]{3,2,1,0:T(8,128)(2,1)}) custom-call(s32[32]{0:T(128)} %get-tuple-element.21.index_ref, bf16[64,2,8,576]{3,2,1,0:T(8,128)(2,1)} %all_to_all.15.rows_ref), custom_call_target="tpu_custom_call" | custom-call | tf_op jit(solution)/shard_map/pick/pallas_call | solution.py:98
  48.6 1.3 copy.19
  50.0 2.0 %collective-permute-start.1 = (bf16[2,256,576]{1,2,0:T(8,128)(2,1)S(1)}, bf16[2,256,576]{1,2,0:T(8,128)(2,1)S(1)}, u32[]{:S(2)}, u32[]{:S(2)}) collective-permute-start(bf16[2,256,576]{1,2,0:T(8,128)(2,1)S(1)} %copy.19), channel_id=1, source_target_pairs={{0,1},{1,2},{2,3},{3,4},{4,5},{5,6},{6,7},{7,0},{8,9},{9,10},{10,1... | collective-permute-start | bytes 1769480 | tf_op jit(solution)/shard_map/ppermute | solution.py:256
  52.0 4.0 %collective-permute-start = (bf16[2,256,576]{1,2,0:T(8,128)(2,1)S(1)}, bf16[2,256,576]{1,2,0:T(8,128)(2,1)S(1)}, u32[]{:S(2)}, u32[]{:S(2)}) collective-permute-start(bf16[2,256,576]{1,2,0:T(8,128)(2,1)S(1)} %copy.19), channel_id=1, source_target_pairs={{0,7},{1,0},{2,1},{3,2},{4,3},{5,4},{6,5},{7,6},{8,15},{9,8},{10,9... | collective-permute-start | bytes 1769480 | tf_op jit(solution)/shard_map/ppermute | solution.py:256
  56.0 4.1 %collective-permute-start.3 = (bf16[256,576]{1,0:T(8,128)(2,1)}, bf16[256,576]{1,0:T(8,128)(2,1)S(1)}, u32[]{:S(2)}, u32[]{:S(2)}) collective-permute-start(bf16[256,576]{1,0:T(8,128)(2,1)} %bitcast.65), channel_id=1, source_target_pairs={{0,6},{1,7},{2,0},{3,1},{4,2},{5,3},{6,4},{7,5},{8,14},{9,15},{10,... | collective-permute-start | bytes 884744 | tf_op jit(solution)/shard_map/ppermute | solution.py:256
  60.1 10.0 %collective-permute-done.1 = bf16[2,256,576]{1,2,0:T(8,128)(2,1)S(1)} collective-permute-done((bf16[2,256,576]{1,2,0:T(8,128)(2,1)S(1)}, bf16[2,256,576]{1,2,0:T(8,128)(2,1)S(1)}, u32[]{:S(2)}, u32[]{:S(2)}) %collective-permute-start.1) | collective-permute-done | bytes 589856 | tf_op jit(solution)/shard_map/ppermute | solution.py:256
  70.1 1.1 copy.22.refs_2_
  71.2 2.2 %collective-permute-done = bf16[2,256,576]{1,2,0:T(8,128)(2,1)S(1)} collective-permute-done((bf16[2,256,576]{1,2,0:T(8,128)(2,1)S(1)}, bf16[2,256,576]{1,2,0:T(8,128)(2,1)S(1)}, u32[]{:S(2)}, u32[]{:S(2)}) %collective-permute-start) | collective-permute-done | bytes 589856 | tf_op jit(solution)/shard_map/ppermute | solution.py:256
  73.4 1.1 copy.21.refs_1_
  74.4 4.2 %collective-permute-done.2.refs_3_ = bf16[256,576]{1,0:T(8,128)(2,1)S(1)} collective-permute-done((bf16[256,576]{1,0:T(8,128)(2,1)}, bf16[256,576]{1,0:T(8,128)(2,1)S(1)}, u32[]{:S(2)}, u32[]{:S(2)}) %collective-permute-start.2) | collective-permute-done | bytes 294944 | tf_op jit(solution)/shard_map/ppermute | solution.py:256
  78.6 4.7 %collective-permute-done.3.refs_4_ = bf16[256,576]{1,0:T(8,128)(2,1)S(1)} collective-permute-done((bf16[256,576]{1,0:T(8,128)(2,1)}, bf16[256,576]{1,0:T(8,128)(2,1)S(1)}, u32[]{:S(2)}, u32[]{:S(2)}) %collective-permute-start.3) | collective-permute-done | bytes 294944 | tf_op jit(solution)/shard_map/ppermute | solution.py:256
  84.1 20.8 %group_grads.1 = (bf16[2,576,1024]{2,1,0:T(8,128)(2,1)}, f32[2,128,576]{2,1,0:T(8,128)}, bf16[128,576]{1,0:T(8,128)(2,1)}, bf16[2,128,576]{2,1,0:T(8,128)(2,1)},...) custom-call(s32[1]{0:T(128)} %bitcast.me_ref, ...), custom_call_target="tpu_custom_call" | custom-call | flops 11542724608 | bytes 15000000 | tf_op jit(solution)/shard_map/group_grads/pallas_call | solution.py:233
  104.8 2.2 %collective-permute-start.6 = (bf16[2,128,576]{2,1,0:T(8,128)(2,1)}, bf16[2,128,576]{2,1,0:T(8,128)(2,1)S(1)}, u32[]{:S(2)}, u32[]{:S(2)}) collective-permute-start(bf16[2,128,576]{2,1,0:T(8,128)(2,1)} %get-tuple-element.35), channel_id=1, source_target_pairs={{0,1},{1,2},{2,3},{3,4},{4,5},{5,6},{6,7},{7,0},{8,9},{9,10},{10,1... | collective-permute-start | bytes 884744 | tf_op jit(solution)/shard_map/ppermute | solution.py:256
  107.0 3.1 %collective-permute-start.7 = (bf16[128,576]{1,0:T(8,128)(2,1)}, bf16[128,576]{1,0:T(8,128)(2,1)S(1)}, u32[]{:S(2)}, u32[]{:S(2)}) collective-permute-start(bf16[128,576]{1,0:T(8,128)(2,1)} %get-tuple-element.36), channel_id=1, source_target_pairs={{0,2},{1,3},{2,4},{3,5},{4,6},{5,7},{6,0},{7,1},{8,10},{9,11},{10,... | collective-permute-start | bytes 442376 | tf_op jit(solution)/shard_map/ppermute | solution.py:256
  110.1 3.1 %collective-permute-start.9 = (bf16[2,128,576]{2,1,0:T(8,128)(2,1)}, bf16[2,128,576]{2,1,0:T(8,128)(2,1)S(1)}, u32[]{:S(2)}, u32[]{:S(2)}) collective-permute-start(bf16[2,128,576]{2,1,0:T(8,128)(2,1)} %get-tuple-element.38), channel_id=1, source_target_pairs={{0,7},{1,0},{2,1},{3,2},{4,3},{5,4},{6,5},{7,6},{8,15},{9,8},{10,9... | collective-permute-start | bytes 884744 | tf_op jit(solution)/shard_map/ppermute | solution.py:256
  113.3 1.5 collective-permute-start.4
  114.7 9.7 %collective-permute-done.7 = bf16[128,576]{1,0:T(8,128)(2,1)S(1)} collective-permute-done((bf16[128,576]{1,0:T(8,128)(2,1)}, bf16[128,576]{1,0:T(8,128)(2,1)S(1)}, u32[]{:S(2)}, u32[]{:S(2)}) %collective-permute-start.7) | collective-permute-done | bytes 147488 | tf_op jit(solution)/shard_map/ppermute | solution.py:256
  124.4 2.9 %collective-permute-start.5 = (bf16[2,128,576]{2,1,0:T(8,128)(2,1)}, bf16[2,128,576]{2,1,0:T(8,128)(2,1)S(1)}, u32[]{:S(2)}, u32[]{:S(2)}) collective-permute-start(bf16[2,128,576]{2,1,0:T(8,128)(2,1)} %get-tuple-element.33), channel_id=1, source_target_pairs={{0,7},{1,0},{2,1},{3,2},{4,3},{5,4},{6,5},{7,6},{8,15},{9,8},{10,9... | collective-permute-start | bytes 884744 | tf_op jit(solution)/shard_map/ppermute | solution.py:256
  127.3 1.1 add_convert_fusion.1
  129.1 4.2 %collective-permute-start.11 = (bf16[2,128,576]{2,1,0:T(8,128)(2,1)S(1)}, bf16[2,128,576]{2,1,0:T(8,128)(2,1)S(1)}, u32[]{:S(2)}, u32[]{:S(2)}) collective-permute-start(bf16[2,128,576]{2,1,0:T(8,128)(2,1)S(1)} %add_convert_fusion), channel_id=1, source_target_pairs={{0,6},{1,7},{2,0},{3,1},{4,2},{5,3},{6,4},{7,5},{8,14},{9,15},{10,... | collective-permute-start | bytes 884744 | tf_op jit(solution)/shard_map/ppermute | solution.py:256
  133.3 5.1 %collective-permute-done.5 = bf16[2,128,576]{2,1,0:T(8,128)(2,1)S(1)} collective-permute-done((bf16[2,128,576]{2,1,0:T(8,128)(2,1)}, bf16[2,128,576]{2,1,0:T(8,128)(2,1)S(1)}, u32[]{:S(2)}, u32[]{:S(2)}) %collective-permute-start.5) | collective-permute-done | bytes 294944 | tf_op jit(solution)/shard_map/ppermute | solution.py:256
  138.4 3.5 %collective-permute-done.8 = bf16[2,128,576]{2,1,0:T(8,128)(2,1)S(1)} collective-permute-done((bf16[2,128,576]{2,1,0:T(8,128)(2,1)S(1)}, bf16[2,128,576]{2,1,0:T(8,128)(2,1)S(1)}, u32[]{:S(2)}, u32[]{:S(2)}) %collective-permute-start.8) | collective-permute-done | bytes 294944 | tf_op jit(solution)/shard_map/ppermute | solution.py:256
  141.9 5.6 %collective-permute-done.11 = bf16[2,128,576]{2,1,0:T(8,128)(2,1)S(1)} collective-permute-done((bf16[2,128,576]{2,1,0:T(8,128)(2,1)S(1)}, bf16[2,128,576]{2,1,0:T(8,128)(2,1)S(1)}, u32[]{:S(2)}, u32[]{:S(2)}) %collective-permute-start.11) | collective-permute-done | bytes 294944 | tf_op jit(solution)/shard_map/ppermute | solution.py:256
  147.5 0.7 copy-done.6
  148.2 2.7 %sum_take.1 = bf16[64,8,576]{2,1,0:T(8,128)(2,1)} custom-call(s32[64]{0:T(128)} %get-tuple-element.30.index_ref, f32[32,8,576]{2,1,0:T(8,128)} %bitcast.57, bf16[32,8,576]{2,1,0:T(8,128)(2,1)} %bitcast.58, bf16[32,8,576]{2,1,0:T(8,128)(2,1)} %bitcast.59, bf16[32,8,576]{2,1,0:T(8,128)(2,1)} %bitcast.60, bf16[32,8,576]{2,1,0:T(8,128)(2,1)} %bitcast.61), custom_call_target="tpu_custom_call" | custom-call | tf_op jit(solution)/shard_map/sum_take/pallas_call | solution.py:119
  151.0 4.8 %all-to-all-start.2 = ((bf16[64,8,576]{2,1,0:T(8,128)(2,1)}), bf16[64,8,576]{2,1,0:T(8,128)(2,1)S(1)}, u32[]{:S(2)}, u32[]{:S(2)}) async-start(bf16[64,8,576]{2,1,0:T(8,128)(2,1)} %sum_take.1), calls=%async_computation.2 | async-start | bytes 1310720 | tf_op jit(solution)/shard_map/all_to_all | solution.py:315
  155.8 3.1 %copy.23 = bf16[2,576,1024]{1,2,0:T(8,128)(2,1)S(1)} copy(bf16[2,576,1024]{2,1,0:T(8,128)(2,1)} %get-tuple-element.29) | data formatting | bytes 4718592 | tf_op jit(solution)/shard_map/group_grads/pallas_call | solution.py:233
  158.9 3.1 %copy.25 = bf16[128,16,576]{0,2,1:T(8,128)(2,1)} copy(bf16[128,16,576]{2,1,0:T(8,128)(2,1)S(1)} %bitcast.50) | data formatting | bytes 4718592
  162.0 5.7 %all-to-all-done.2.rows_ref = bf16[64,8,576]{2,1,0:T(8,128)(2,1)S(1)} async-done(((bf16[64,8,576]{2,1,0:T(8,128)(2,1)}), bf16[64,8,576]{2,1,0:T(8,128)(2,1)S(1)}, u32[]{:S(2)}, u32[]{:S(2)}) %all-to-all-start.2) | async-done | bytes 589856 | tf_op jit(solution)/shard_map/all_to_all | solution.py:315
  167.7 0.8 copy-done
  168.5 2.1 %gather_sum.1 = bf16[8,8,576]{2,1,0:T(8,128)(2,1)} custom-call(s32[32,1,2]{2,1,0:T(1,128)} %copy-done.7, bf16[64,8,576]{2,1,0:T(8,128)(2,1)} %copy-done), custom_call_target="tpu_custom_call" | custom-call | tf_op jit(solution)/shard_map/gather_sum/pallas_call | solution.py:140
  170.7 3.5 %collective-permute-start.15 = (bf16[8,8,576]{2,1,0:T(8,128)(2,1)}, bf16[8,8,576]{2,1,0:T(8,128)(2,1)S(1)}, u32[]{:S(2)}, u32[]{:S(2)}) collective-permute-start(bf16[8,8,576]{2,1,0:T(8,128)(2,1)} %gather_sum.1), channel_id=1, source_target_pairs={{0,2},{1,3},{2,4},{3,5},{4,6},{5,7},{6,0},{7,1},{8,10},{9,11},{10,... | collective-permute-start | bytes 221192 | tf_op jit(solution)/shard_map/ppermute | solution.py:256
  174.1 1.2 collective-permute-start.13
  175.3 2.0 %collective-permute-start.12 = (bf16[8,8,576]{2,1,0:T(8,128)(2,1)}, bf16[8,8,576]{2,1,0:T(8,128)(2,1)S(1)}, u32[]{:S(2)}, u32[]{:S(2)}) collective-permute-start(bf16[8,8,576]{2,1,0:T(8,128)(2,1)} %gather_sum.1), channel_id=1, source_target_pairs={{0,7},{1,0},{2,1},{3,2},{4,3},{5,4},{6,5},{7,6},{8,15},{9,8},{10,9... | collective-permute-start | bytes 221192 | tf_op jit(solution)/shard_map/ppermute | solution.py:256
  177.4 0.9 bitcast_dynamic-update-slice_fusion.14
  178.3 2.0 %collective-permute-done.15 = bf16[8,8,576]{2,1,0:T(8,128)(2,1)S(1)} collective-permute-done((bf16[8,8,576]{2,1,0:T(8,128)(2,1)}, bf16[8,8,576]{2,1,0:T(8,128)(2,1)S(1)}, u32[]{:S(2)}, u32[]{:S(2)}) %collective-permute-start.15) | collective-permute-done | bytes 73760 | tf_op jit(solution)/shard_map/ppermute | solution.py:256
  180.3 2.8 %collective-permute-start.17 = (bf16[8,8,576]{2,1,0:T(8,128)(2,1)S(1)}, bf16[8,8,576]{2,1,0:T(8,128)(2,1)S(1)}, u32[]{:S(2)}, u32[]{:S(2)}) collective-permute-start(bf16[8,8,576]{2,1,0:T(8,128)(2,1)S(1)} %collective-permute-done.15), channel_id=1, source_target_pairs={{0,1},{1,2},{2,3},{3,4},{4,5},{5,6},{6,7},{7,0},{8,9},{9,10},{10,1... | collective-permute-start | bytes 221192 | tf_op jit(solution)/shard_map/ppermute | solution.py:256
  183.1 0.8 collective-permute-start.16
  184.0 1.8 collective-permute-start.14
  185.8 2.6 %collective-permute-done.14 = bf16[8,8,576]{2,1,0:T(8,128)(2,1)S(1)} collective-permute-done((bf16[8,8,576]{2,1,0:T(8,128)(2,1)S(1)}, bf16[8,8,576]{2,1,0:T(8,128)(2,1)S(1)}, u32[]{:S(2)}, u32[]{:S(2)}) %collective-permute-start.14) | collective-permute-done | bytes 73760 | tf_op jit(solution)/shard_map/ppermute | solution.py:256
  188.4 2.5 %collective-permute-done.16 = bf16[8,8,576]{2,1,0:T(8,128)(2,1)S(1)} collective-permute-done((bf16[8,8,576]{2,1,0:T(8,128)(2,1)S(1)}, bf16[8,8,576]{2,1,0:T(8,128)(2,1)S(1)}, u32[]{:S(2)}, u32[]{:S(2)}) %collective-permute-start.16) | collective-permute-done | bytes 73760 | tf_op jit(solution)/shard_map/ppermute | solution.py:256
  191.4 1.4 copy.26
  (50 shorter events, 3.2 us)
Async XLA Ops:
  2.5 14.6 %all-to-all-start = ((s32[32,1,2]{2,1,0:T(1,128)}), s32[32,1,2]{2,1,0:T(1,128)S(1)}, u32[]{:S(2)}, u32[]{:S(2)}) async-start(s32[32,1,2]{2,1,0:T(1,128)} %get-tuple-element.22), calls=%async_computation | async-start | bytes 32768 | tf_op jit(solution)/shard_map/all_to_all | solution.py:291
  17.1 0.6 copy-start.7
  50.0 20.1 %collective-permute-start.1 = (bf16[2,256,576]{1,2,0:T(8,128)(2,1)S(1)}, bf16[2,256,576]{1,2,0:T(8,128)(2,1)S(1)}, u32[]{:S(2)}, u32[]{:S(2)}) collective-permute-start(bf16[2,256,576]{1,2,0:T(8,128)(2,1)S(1)} %copy.19), channel_id=1, source_target_pairs={{0,1},{1,2},{2,3},{3,4},{4,5},{5,6},{6,7},{7,0},{8,9},{9,10},{10,1... | collective-permute-start | bytes 1769480 | tf_op jit(solution)/shard_map/ppermute | solution.py:256
  52.0 21.4 %collective-permute-start = (bf16[2,256,576]{1,2,0:T(8,128)(2,1)S(1)}, bf16[2,256,576]{1,2,0:T(8,128)(2,1)S(1)}, u32[]{:S(2)}, u32[]{:S(2)}) collective-permute-start(bf16[2,256,576]{1,2,0:T(8,128)(2,1)S(1)} %copy.19), channel_id=1, source_target_pairs={{0,7},{1,0},{2,1},{3,2},{4,3},{5,4},{6,5},{7,6},{8,15},{9,8},{10,9... | collective-permute-start | bytes 1769480 | tf_op jit(solution)/shard_map/ppermute | solution.py:256
  56.0 22.6 %collective-permute-start.2 = (bf16[256,576]{1,0:T(8,128)(2,1)}, bf16[256,576]{1,0:T(8,128)(2,1)S(1)}, u32[]{:S(2)}, u32[]{:S(2)}) collective-permute-start(bf16[256,576]{1,0:T(8,128)(2,1)} %bitcast.66), channel_id=1, source_target_pairs={{0,2},{1,3},{2,4},{3,5},{4,6},{5,7},{6,0},{7,1},{8,10},{9,11},{10,... | collective-permute-start | bytes 884744 | tf_op jit(solution)/shard_map/ppermute | solution.py:256
  56.0 27.3 %collective-permute-start.3 = (bf16[256,576]{1,0:T(8,128)(2,1)}, bf16[256,576]{1,0:T(8,128)(2,1)S(1)}, u32[]{:S(2)}, u32[]{:S(2)}) collective-permute-start(bf16[256,576]{1,0:T(8,128)(2,1)} %bitcast.65), channel_id=1, source_target_pairs={{0,6},{1,7},{2,0},{3,1},{4,2},{5,3},{6,4},{7,5},{8,14},{9,15},{10,... | collective-permute-start | bytes 884744 | tf_op jit(solution)/shard_map/ppermute | solution.py:256
  78.6 4.7 %copy-start.8 = (bf16[256,576]{1,0:T(8,128)(2,1)}, bf16[256,576]{1,0:T(8,128)(2,1)S(1)}, u32[]{:S(2)}) copy-start(bf16[256,576]{1,0:T(8,128)(2,1)S(1)} %collective-permute-done.2.refs_3_) | copy-start | bytes 884740
  83.3 0.7 copy-start.9
  104.8 24.1 %copy-start.2 = (bf16[2,128,576]{2,1,0:T(8,128)(2,1)S(1)}, bf16[2,128,576]{2,1,0:T(8,128)(2,1)}, u32[]{:S(2)}) copy-start(bf16[2,128,576]{2,1,0:T(8,128)(2,1)} %get-tuple-element.37) | copy-start | bytes 884740
  104.8 22.4 %collective-permute-start.6 = (bf16[2,128,576]{2,1,0:T(8,128)(2,1)}, bf16[2,128,576]{2,1,0:T(8,128)(2,1)S(1)}, u32[]{:S(2)}, u32[]{:S(2)}) collective-permute-start(bf16[2,128,576]{2,1,0:T(8,128)(2,1)} %get-tuple-element.35), channel_id=1, source_target_pairs={{0,1},{1,2},{2,3},{3,4},{4,5},{5,6},{6,7},{7,0},{8,9},{9,10},{10,1... | collective-permute-start | bytes 884744 | tf_op jit(solution)/shard_map/ppermute | solution.py:256
  107.0 17.4 %collective-permute-start.7 = (bf16[128,576]{1,0:T(8,128)(2,1)}, bf16[128,576]{1,0:T(8,128)(2,1)S(1)}, u32[]{:S(2)}, u32[]{:S(2)}) collective-permute-start(bf16[128,576]{1,0:T(8,128)(2,1)} %get-tuple-element.36), channel_id=1, source_target_pairs={{0,2},{1,3},{2,4},{3,5},{4,6},{5,7},{6,0},{7,1},{8,10},{9,11},{10,... | collective-permute-start | bytes 442376 | tf_op jit(solution)/shard_map/ppermute | solution.py:256
  110.1 18.8 %collective-permute-start.9 = (bf16[2,128,576]{2,1,0:T(8,128)(2,1)}, bf16[2,128,576]{2,1,0:T(8,128)(2,1)S(1)}, u32[]{:S(2)}, u32[]{:S(2)}) collective-permute-start(bf16[2,128,576]{2,1,0:T(8,128)(2,1)} %get-tuple-element.38), channel_id=1, source_target_pairs={{0,7},{1,0},{2,1},{3,2},{4,3},{5,4},{6,5},{7,6},{8,15},{9,8},{10,9... | collective-permute-start | bytes 884744 | tf_op jit(solution)/shard_map/ppermute | solution.py:256
  113.3 15.7 %collective-permute-start.10 = (bf16[128,576]{1,0:T(8,128)(2,1)}, bf16[128,576]{1,0:T(8,128)(2,1)S(1)}, u32[]{:S(2)}, u32[]{:S(2)}) collective-permute-start(bf16[128,576]{1,0:T(8,128)(2,1)} %get-tuple-element.39), channel_id=1, source_target_pairs={{0,6},{1,7},{2,0},{3,1},{4,2},{5,3},{6,4},{7,5},{8,14},{9,15},{10,... | collective-permute-start | bytes 442376 | tf_op jit(solution)/shard_map/ppermute | solution.py:256
  113.3 20.0 %collective-permute-start.4 = (bf16[2,128,576]{2,1,0:T(8,128)(2,1)}, bf16[2,128,576]{2,1,0:T(8,128)(2,1)S(1)}, u32[]{:S(2)}, u32[]{:S(2)}) collective-permute-start(bf16[2,128,576]{2,1,0:T(8,128)(2,1)} %get-tuple-element.32), channel_id=1, source_target_pairs={{0,1},{1,2},{2,3},{3,4},{4,5},{5,6},{6,7},{7,0},{8,9},{9,10},{10,1... | collective-permute-start | bytes 884744 | tf_op jit(solution)/shard_map/ppermute | solution.py:256
  124.4 14.0 %collective-permute-start.5 = (bf16[2,128,576]{2,1,0:T(8,128)(2,1)}, bf16[2,128,576]{2,1,0:T(8,128)(2,1)S(1)}, u32[]{:S(2)}, u32[]{:S(2)}) collective-permute-start(bf16[2,128,576]{2,1,0:T(8,128)(2,1)} %get-tuple-element.33), channel_id=1, source_target_pairs={{0,7},{1,0},{2,1},{3,2},{4,3},{5,4},{6,5},{7,6},{8,15},{9,8},{10,9... | collective-permute-start | bytes 884744 | tf_op jit(solution)/shard_map/ppermute | solution.py:256
  128.4 13.5 %collective-permute-start.8 = (bf16[2,128,576]{2,1,0:T(8,128)(2,1)S(1)}, bf16[2,128,576]{2,1,0:T(8,128)(2,1)S(1)}, u32[]{:S(2)}, u32[]{:S(2)}) collective-permute-start(bf16[2,128,576]{2,1,0:T(8,128)(2,1)S(1)} %add_convert_fusion.1), channel_id=1, source_target_pairs={{0,2},{1,3},{2,4},{3,5},{4,6},{5,7},{6,0},{7,1},{8,10},{9,11},{10,... | collective-permute-start | bytes 884744 | tf_op jit(solution)/shard_map/ppermute | solution.py:256
  129.1 18.4 %collective-permute-start.11 = (bf16[2,128,576]{2,1,0:T(8,128)(2,1)S(1)}, bf16[2,128,576]{2,1,0:T(8,128)(2,1)S(1)}, u32[]{:S(2)}, u32[]{:S(2)}) collective-permute-start(bf16[2,128,576]{2,1,0:T(8,128)(2,1)S(1)} %add_convert_fusion), channel_id=1, source_target_pairs={{0,6},{1,7},{2,0},{3,1},{4,2},{5,3},{6,4},{7,5},{8,14},{9,15},{10,... | collective-permute-start | bytes 884744 | tf_op jit(solution)/shard_map/ppermute | solution.py:256
  133.3 14.2 %copy-start.3 = (bf16[2,128,576]{2,1,0:T(8,128)(2,1)}, bf16[2,128,576]{2,1,0:T(8,128)(2,1)S(1)}, u32[]{:S(2)}) copy-start(bf16[2,128,576]{2,1,0:T(8,128)(2,1)S(1)} %collective-permute-done.4) | copy-start | bytes 884740
  138.4 9.1 %copy-start.4 = (bf16[2,128,576]{2,1,0:T(8,128)(2,1)}, bf16[2,128,576]{2,1,0:T(8,128)(2,1)S(1)}, u32[]{:S(2)}) copy-start(bf16[2,128,576]{2,1,0:T(8,128)(2,1)S(1)} %collective-permute-done.5) | copy-start | bytes 884740
  141.9 5.6 %copy-start.5 = (bf16[2,128,576]{2,1,0:T(8,128)(2,1)}, bf16[2,128,576]{2,1,0:T(8,128)(2,1)S(1)}, u32[]{:S(2)}) copy-start(bf16[2,128,576]{2,1,0:T(8,128)(2,1)S(1)} %collective-permute-done.8) | copy-start | bytes 884740
  147.5 0.7 copy-start.6
  151.0 16.7 %all-to-all-start.2 = ((bf16[64,8,576]{2,1,0:T(8,128)(2,1)}), bf16[64,8,576]{2,1,0:T(8,128)(2,1)S(1)}, u32[]{:S(2)}, u32[]{:S(2)}) async-start(bf16[64,8,576]{2,1,0:T(8,128)(2,1)} %sum_take.1), calls=%async_computation.2 | async-start | bytes 1310720 | tf_op jit(solution)/shard_map/all_to_all | solution.py:315
  167.7 0.8 copy-start
  170.7 20.4 %copy-start.1 = (bf16[8,8,576]{2,1,0:T(8,128)(2,1)S(1)}, bf16[8,8,576]{2,1,0:T(8,128)(2,1)}, u32[]{:S(2)}) copy-start(bf16[8,8,576]{2,1,0:T(8,128)(2,1)} %gather_sum.1) | copy-start | bytes 221188
  170.7 20.3 %collective-permute-start.18 = (bf16[8,8,576]{2,1,0:T(8,128)(2,1)}, bf16[8,8,576]{2,1,0:T(8,128)(2,1)S(1)}, u32[]{:S(2)}, u32[]{:S(2)}) collective-permute-start(bf16[8,8,576]{2,1,0:T(8,128)(2,1)} %gather_sum.1), channel_id=1, source_target_pairs={{0,1},{1,2},{2,3},{3,4},{4,5},{5,6},{6,7},{7,0},{8,9},{9,10},{10,1... | collective-permute-start | bytes 221192 | tf_op jit(solution)/shard_map/ppermute | solution.py:256
  170.7 9.6 %collective-permute-start.15 = (bf16[8,8,576]{2,1,0:T(8,128)(2,1)}, bf16[8,8,576]{2,1,0:T(8,128)(2,1)S(1)}, u32[]{:S(2)}, u32[]{:S(2)}) collective-permute-start(bf16[8,8,576]{2,1,0:T(8,128)(2,1)} %gather_sum.1), channel_id=1, source_target_pairs={{0,2},{1,3},{2,4},{3,5},{4,6},{5,7},{6,0},{7,1},{8,10},{9,11},{10,... | collective-permute-start | bytes 221192 | tf_op jit(solution)/shard_map/ppermute | solution.py:256
  174.1 9.8 %collective-permute-start.13 = (bf16[8,8,576]{2,1,0:T(8,128)(2,1)}, bf16[8,8,576]{2,1,0:T(8,128)(2,1)S(1)}, u32[]{:S(2)}, u32[]{:S(2)}) collective-permute-start(bf16[8,8,576]{2,1,0:T(8,128)(2,1)} %gather_sum.1), channel_id=1, source_target_pairs={{0,6},{1,7},{2,0},{3,1},{4,2},{5,3},{6,4},{7,5},{8,14},{9,15},{10,... | collective-permute-start | bytes 221192 | tf_op jit(solution)/shard_map/ppermute | solution.py:256
  175.3 10.5 %collective-permute-start.12 = (bf16[8,8,576]{2,1,0:T(8,128)(2,1)}, bf16[8,8,576]{2,1,0:T(8,128)(2,1)S(1)}, u32[]{:S(2)}, u32[]{:S(2)}) collective-permute-start(bf16[8,8,576]{2,1,0:T(8,128)(2,1)} %gather_sum.1), channel_id=1, source_target_pairs={{0,7},{1,0},{2,1},{3,2},{4,3},{5,4},{6,5},{7,6},{8,15},{9,8},{10,9... | collective-permute-start | bytes 221192 | tf_op jit(solution)/shard_map/ppermute | solution.py:256
  180.3 10.6 %collective-permute-start.17 = (bf16[8,8,576]{2,1,0:T(8,128)(2,1)S(1)}, bf16[8,8,576]{2,1,0:T(8,128)(2,1)S(1)}, u32[]{:S(2)}, u32[]{:S(2)}) collective-permute-start(bf16[8,8,576]{2,1,0:T(8,128)(2,1)S(1)} %collective-permute-done.15), channel_id=1, source_target_pairs={{0,1},{1,2},{2,3},{3,4},{4,5},{5,6},{6,7},{7,0},{8,9},{9,10},{10,1... | collective-permute-start | bytes 221192 | tf_op jit(solution)/shard_map/ppermute | solution.py:256
  183.1 7.8 %collective-permute-start.16 = (bf16[8,8,576]{2,1,0:T(8,128)(2,1)S(1)}, bf16[8,8,576]{2,1,0:T(8,128)(2,1)S(1)}, u32[]{:S(2)}, u32[]{:S(2)}) collective-permute-start(bf16[8,8,576]{2,1,0:T(8,128)(2,1)S(1)} %collective-permute-done.15), channel_id=1, source_target_pairs={{0,2},{1,3},{2,4},{3,5},{4,6},{5,7},{6,0},{7,1},{8,10},{9,11},{10,... | collective-permute-start | bytes 221192 | tf_op jit(solution)/shard_map/ppermute | solution.py:256
  184.0 4.4 %collective-permute-start.14 = (bf16[8,8,576]{2,1,0:T(8,128)(2,1)S(1)}, bf16[8,8,576]{2,1,0:T(8,128)(2,1)S(1)}, u32[]{:S(2)}, u32[]{:S(2)}) collective-permute-start(bf16[8,8,576]{2,1,0:T(8,128)(2,1)S(1)} %collective-permute-done.13), channel_id=1, source_target_pairs={{0,7},{1,0},{2,1},{3,2},{4,3},{5,4},{6,5},{7,6},{8,15},{9,8},{10,9... | collective-permute-start | bytes 221192 | tf_op jit(solution)/shard_map/ppermute | solution.py:256

commit v2 on v0

v2 whole, which is shorter than its diff:
```python
import functools

import jax
import jax.numpy as jnp
from jax import lax
from jax.experimental import pallas as pl
from jax.experimental.pallas import tpu as pltpu
from jax.sharding import PartitionSpec as P

BLK = 64
CAPACITY = 2
LOG2E = 1.4426950408889634
softmax_scale = 192.0 ** (-0.5)
VMEM_LIMIT = 56 * 1024 * 1024
ROWS_BY_ROWS = (((1,), (1,)), ((), ()))
COLS_BY_COLS = (((0,), (0,)), ((), ()))
OFFSETS = (0, 1, -1, 2, -2, 3, -3, 4)


def smem():
    return pl.BlockSpec(memory_space=pltpu.SMEM)


def vmem():
    return pl.BlockSpec(memory_space=pltpu.VMEM)


def one_hot(hit):
    return jnp.where(hit, 1.0, 0.0).astype(jnp.bfloat16)


def plan_kernel(stored_blocks, lists_ref, home_ref, entry_ref, count):
    groups, chosen = lists_ref.shape
    for owner in range(count.shape[0]):
        count[owner] = 0
    for slot in range(entry_ref.shape[0]):
        entry_ref[slot] = 0
    for group in range(groups):
        for at in range(chosen):
            owner = home_ref[lists_ref[group, at]] // stored_blocks
            earlier = count[owner]
            entry_ref[owner * CAPACITY + earlier] = group * chosen + at
            count[owner] = earlier + 1


def plan(block_lists, block_home, ctx_count, stored_blocks):
    return pl.pallas_call(
        functools.partial(plan_kernel, stored_blocks),
        out_shape=jax.ShapeDtypeStruct((ctx_count * CAPACITY,), jnp.int32),
        in_specs=[smem(), smem()],
        out_specs=smem(),
        scratch_shapes=[pltpu.SMEM((ctx_count,), jnp.int32)],
        name="plan",
    )(block_lists, block_home)


def spread_kernel(pair, lists_ref, home_ref, latent_ref, out_ref):
    width, tokens = latent_ref.shape
    stored = tokens // BLK
    span = stored * pair
    row = lax.broadcasted_iota(jnp.int32, (tokens, tokens), 0)
    col = lax.broadcasted_iota(jnp.int32, (tokens, tokens), 1)
    source = (row % span) // pair * BLK + row // span * pair + row % pair
    moved = lax.dot_general(
        one_hot(col == source),
        latent_ref[...],
        ROWS_BY_ROWS,
        preferred_element_type=jnp.float32,
    )
    out_ref[:, :width] = moved.astype(out_ref.dtype)
    free = out_ref.shape[1] - width
    entry = lax.broadcasted_iota(jnp.int32, (span, free), 0) // pair
    entry = entry + stored * lax.broadcasted_iota(jnp.int32, (span, free), 1)
    groups, chosen = lists_ref.shape
    value = jnp.zeros((span, free), jnp.float32)
    for group in range(groups):
        for at in range(chosen):
            position = home_ref[lists_ref[group, at]].astype(jnp.float32)
            value = jnp.where(entry == group * chosen + at, position, value)
    value = value.astype(out_ref.dtype)
    for start in range(0, tokens, span):
        out_ref[start : start + span, width:] = value


def spread(block_lists, block_home, latent_cols, pair):
    width, tokens = latent_cols.shape
    return pl.pallas_call(
        functools.partial(spread_kernel, pair),
        out_shape=jax.ShapeDtypeStruct((tokens, 640), latent_cols.dtype),
        in_specs=[smem(), smem(), vmem()],
        out_specs=vmem(),
        compiler_params=pltpu.CompilerParams(vmem_limit_bytes=VMEM_LIMIT),
        name="spread",
    )(block_lists, block_home, latent_cols)


def choose_kernel(pair, held_ref, out_ref):
    targets, steps, span, width = out_ref.shape
    count = held_ref.shape[0]
    rows = held_ref[:, :width]
    lists = held_ref[:, width:].astype(jnp.float32)
    parity = lax.broadcasted_iota(jnp.int32, (count, 1), 0) % pair
    col = lax.broadcasted_iota(jnp.int32, (count, count), 1).astype(jnp.float32)
    for step in range(steps):
        source = lists[:, step : step + 1] * pair + parity.astype(jnp.float32)
        chosen = jnp.dot(one_hot(col == source), rows, preferred_element_type=jnp.float32)
        out_ref[:, step] = chosen.astype(out_ref.dtype).reshape(targets, span, width)


def choose(held, width, targets, entries, pair):
    span = held.shape[0] // targets
    steps = entries * pair // span
    return pl.pallas_call(
        functools.partial(choose_kernel, pair),
        out_shape=jax.ShapeDtypeStruct((targets, steps, span, width), held.dtype),
        in_specs=[vmem()],
        out_specs=vmem(),
        compiler_params=pltpu.CompilerParams(vmem_limit_bytes=VMEM_LIMIT),
        name="choose",
    )(held)


def place_kernel(pair, index_ref, *refs):
    term_refs, out_ref, total, picks = refs[:-3], refs[-3], refs[-2], refs[-1]
    half = len(term_refs) // 2
    rows = term_refs[0].shape[0]
    share = out_ref.shape[1]
    spread_over = rows * pair // share
    for group in range(2):
        terms = term_refs[group * half : (group + 1) * half]
        value = terms[0][...].astype(jnp.float32)
        for term in terms[1:]:
            value = value + term[...].astype(jnp.float32)
        total[group * rows : (group + 1) * rows, :] = value.astype(total.dtype)
    row = lax.broadcasted_iota(jnp.int32, (share, 2 * rows), 0)
    col = lax.broadcasted_iota(jnp.int32, (share, 2 * rows), 1)
    lead = col - (row // pair * spread_over + row % pair)
    chosen = spread_over // pair
    for slot in range(out_ref.shape[0]):
        entry = index_ref[slot]
        start = entry // chosen * rows + entry % chosen * pair
        picks[slot * share : (slot + 1) * share, :] = jnp.where(lead == start, 1.0, 0.0)
    placed = jnp.dot(
        picks[...].astype(jnp.bfloat16), total[...], preferred_element_type=jnp.float32
    )
    out_ref[...] = placed.astype(out_ref.dtype).reshape(out_ref.shape)


def place(index, by_group, share, pair):
    terms = [term for group in by_group for term in group]
    rows, width = terms[0].shape
    slots = index.shape[0]
    return pl.pallas_call(
        functools.partial(place_kernel, pair),
        out_shape=jax.ShapeDtypeStruct((slots, share, width), jnp.bfloat16),
        in_specs=[smem()] + [vmem()] * len(terms),
        out_specs=vmem(),
        scratch_shapes=[
            pltpu.VMEM((2 * rows, width), jnp.bfloat16),
            pltpu.VMEM((slots * share, 2 * rows), jnp.float32),
        ],
        name="place",
    )(index, *terms)


def gather_sum_kernel(index_ref, rows_ref, out_ref, total):
    total[...] = jnp.zeros_like(total)
    stored = out_ref.shape[0]
    for at in range(rows_ref.shape[0]):
        index = index_ref[at]
        index = jnp.where(index < 0, stored, index)
        total[index] += rows_ref[at].astype(jnp.float32)
    out_ref[...] = total[:stored].astype(out_ref.dtype)


def gather_sum(index, rows, stored):
    return pl.pallas_call(
        gather_sum_kernel,
        out_shape=jax.ShapeDtypeStruct((stored,) + rows.shape[1:], jnp.bfloat16),
        in_specs=[smem(), vmem()],
        out_specs=vmem(),
        scratch_shapes=[pltpu.VMEM((stored + 1,) + rows.shape[1:], jnp.float32)],
        name="gather_sum",
    )(index, rows)


def group_kernel(me_ref, key_ref, query_ref, grad_ref, query_out, *refs):
    part_refs, sums = refs[:-1], refs[-1]
    step = pl.program_id(0)
    width = query_ref.shape[1]
    value_width = grad_ref.shape[1]
    keys = key_ref[...].reshape(sums.shape)

    scores = lax.dot_general(
        keys, query_ref[...], ROWS_BY_ROWS, preferred_element_type=jnp.float32
    )
    factor = softmax_scale * LOG2E
    top = jnp.max(scores, axis=0, keepdims=True) * factor
    raised = jnp.exp2(scores * factor - top)
    weights = raised * (1.0 / jnp.sum(raised, axis=0, keepdims=True))
    half = weights.astype(jnp.bfloat16)
    weight_grad = lax.dot_general(
        keys[:, :value_width], grad_ref[...], ROWS_BY_ROWS, preferred_element_type=jnp.float32
    )
    delta = jnp.sum(half.astype(jnp.float32) * weight_grad, axis=0, keepdims=True)
    score_half = (weights * (weight_grad - delta)).astype(jnp.bfloat16)
    from_scores = (
        jnp.dot(score_half, query_ref[...], preferred_element_type=jnp.float32) * softmax_scale
    )
    from_values = jnp.dot(half, grad_ref[...], preferred_element_type=jnp.float32)
    sums[:, :value_width] = from_scores[:, :value_width] + from_values
    sums[:, value_width:] = from_scores[:, value_width:]
    query_out[...] = (
        lax.dot_general(keys, score_half, COLS_BY_COLS, preferred_element_type=jnp.float32)
        * softmax_scale
    ).astype(jnp.bfloat16)

    me = me_ref[0]
    count = len(OFFSETS)
    part = sums.shape[0] // count
    for group in range(2):

        @pl.when(step == group)
        def _():
            for at, offset in enumerate(OFFSETS):
                start = pl.multiple_of((me + offset + count) % count * part, part)
                out = part_refs[group * count + at]
                out[...] = sums[pl.ds(start, part), :].astype(out.dtype)


def group_grads(me, keys, query_rows, grad_rows):
    sources, groups, span, width = keys.shape
    rows, value_width = grad_rows.shape[1:]
    key_count = sources * span
    part = key_count // len(OFFSETS)
    by_group = lambda *shape: pl.BlockSpec((None,) + shape, lambda i: (i, 0, 0))
    out_shape = [jax.ShapeDtypeStruct((groups, width, rows), jnp.bfloat16)]
    out_specs = [by_group(width, rows)]
    for _ in range(groups):
        for offset in OFFSETS:
            kind = jnp.float32 if offset == 0 else jnp.bfloat16
            out_shape.append(jax.ShapeDtypeStruct((part, width), kind))
            out_specs.append(pl.BlockSpec((part, width), lambda i: (0, 0)))
    flops = 2 * groups * rows * key_count * (3 * width + 2 * value_width)
    return pl.pallas_call(
        group_kernel,
        grid=(groups,),
        in_specs=[
            smem(),
            pl.BlockSpec((sources, None, span, width), lambda i: (0, i, 0, 0)),
            by_group(rows, width),
            by_group(rows, value_width),
        ],
        out_specs=out_specs,
        out_shape=out_shape,
        scratch_shapes=[pltpu.VMEM((key_count, width), jnp.float32)],
        compiler_params=pltpu.CompilerParams(vmem_limit_bytes=VMEM_LIMIT),
        cost_estimate=pl.CostEstimate(
            flops=flops, bytes_accessed=15_000_000, transcendentals=groups * rows * key_count
        ),
        name="group_grads",
    )(me, keys, query_rows, grad_rows)


def shift(x, by):
    count = lax.axis_size("head")
    return lax.ppermute(x, "head", [(i, (i + by) % count) for i in range(count)])


def add(a, b):
    return (a.astype(jnp.float32) + b.astype(jnp.float32)).astype(jnp.bfloat16)


def ring_scatter(parts, group):
    if group == 0:
        right, left = shift(parts[4], 1), shift(parts[-3], -1)
        right = shift(add(parts[3], right), 1)
        left = shift(add(parts[-2], left), -1)
        right = shift(add(parts[2], right), 1)
        left = shift(add(parts[-1], left), -1)
        right = shift(add(parts[1], right), 1)
    else:
        right, left = shift(parts[3], 1), shift(parts[4], -1)
        right = shift(add(parts[2], right), 1)
        left = shift(add(parts[-3], left), -1)
        right = shift(add(parts[1], right), 1)
        left = shift(add(parts[-2], left), -1)
        left = shift(add(parts[-1], left), -1)
    return parts[0], right, left


def requested(lists, me, stored_blocks):
    entry = lax.broadcasted_iota(jnp.int32, lists.shape, 1)
    code = entry * stored_blocks + lists % stored_blocks
    hit = lists // stored_blocks == me
    first = jnp.min(jnp.where(hit, code, 1 << 20), axis=1)
    last = jnp.max(jnp.where(hit, code, -1), axis=1)
    one = jnp.where(last >= 0, first % stored_blocks, -1)
    two = jnp.where(last > first, last % stored_blocks, -1)
    return jnp.stack([one, two], axis=1).reshape(-1)


def local(queries, out_grads, latent, block_lists, block_home):
    ctx_count = lax.axis_size("ctx")
    head_count = lax.axis_size("head")
    me = lax.axis_index("head")
    groups, chosen = block_lists.shape
    tokens, heads, width = queries.shape
    value_width = out_grads.shape[2]
    group_rows = tokens // groups
    stored_blocks = latent.shape[0] // BLK
    entries = groups * chosen
    share = BLK // head_count
    pair = BLK // ctx_count
    span = stored_blocks * pair
    rows = group_rows * heads

    spread_rows = spread(block_lists, block_home, latent.T, pair)
    held = lax.all_to_all(
        spread_rows.reshape(ctx_count, span, 640), "ctx", split_axis=0, concat_axis=0, tiled=True
    )
    query_rows = queries.reshape(groups, rows, width)
    grad_rows = out_grads.reshape(groups, rows, value_width)
    entry_of = plan(block_lists, block_home, ctx_count, stored_blocks)
    held, query_rows, entry_of = lax.optimization_barrier((held, query_rows, entry_of))

    outgoing = choose(held.reshape(ctx_count * span, 640), width, ctx_count, entries, pair)
    outgoing = outgoing.reshape(ctx_count, groups, chosen * pair, width)
    keys = lax.all_to_all(outgoing, "ctx", split_axis=0, concat_axis=0, tiled=True)

    lists = held[:, ::pair, width : width + entries * pair // span].astype(jnp.int32)
    lists = lists.transpose(0, 2, 1).reshape(ctx_count, entries)
    requests_in = requested(lists, lax.axis_index("ctx"), stored_blocks)

    me_ref = me.astype(jnp.int32).reshape(1)
    query_cols, *parts = group_grads(me_ref, keys, query_rows, grad_rows)
    by_group = []
    for group in range(groups):
        terms = parts[group * len(OFFSETS) : (group + 1) * len(OFFSETS)]
        by_group.append(ring_scatter(dict(zip(OFFSETS, terms)), group))
    query_grads = query_cols.reshape(groups, width, group_rows, heads)
    query_grads = query_grads.transpose(0, 2, 3, 1).reshape(tokens, heads, width)

    returned = lax.all_to_all(
        place(entry_of, by_group, share, pair), "ctx", split_axis=0, concat_axis=0, tiled=True
    )
    total = gather_sum(requests_in, returned, stored_blocks)

    minus1, minus2 = shift(total, 1), shift(total, 2)
    plus1, plus2 = shift(total, -1), shift(total, -2)
    minus3, plus3, minus4 = shift(minus2, 1), shift(plus2, -1), shift(minus2, 2)
    pieces = jnp.stack([total, plus1, plus2, plus3, minus4, minus3, minus2, minus1])
    pieces = jnp.roll(pieces, me, axis=0)
    latent_grads = pieces.transpose(1, 0, 2, 3).reshape(stored_blocks * BLK, width)
    return query_grads, latent_grads.astype(jnp.float32)


def solution(mesh):
    in_specs = (P("ctx", "head", None), P("ctx", "head", None), P("ctx", None), P("ctx", None), P())
    out_specs = (P("ctx", "head", None), P("ctx", None))
    return jax.shard_map(local, mesh=mesh, in_specs=in_specs, out_specs=out_specs, check_vma=False)
```

time: 182 us -> 176 us (0.967)
  blocking collectives: 26.4 us -> 0 us
  waiting for transfers between devices: 44 us -> 58.9 us
  local copies, waits for them, and re-layouts: 22.2 us -> 18 us
  Pallas kernels: 30.3 us -> 34 us
  other arithmetic: 1.28 us -> 4.58 us
  starting transfers between devices: 55.2 us -> 58 us
    all_to_all x2 -> x3, waiting for transfers between devices: 5.79 us -> 43.5 us  [the longest x1 33.9 us: local(): lax.all_to_all(outgoing, 'ctx', split_axis=0, concat_axis=0, tiled=True)]
    all_to_all x1 -> x0, blocking collectives: 26.4 us -> none  [local(): lax.all_to_all(take(requests_in, mine), 'ctx', split_axis=0, concat_axis=...]
    ppermute x27 -> x21, waiting for transfers between devices: 38.2 us -> 15.4 us  [shift(): lax.ppermute(x, 'head', [(i, (i + by) % count) for i in range(count)])]
    all_to_all x2 -> x3, starting transfers between devices: 12.6 us -> 20.6 us  [the longest x1 7.76 us: local(): lax.all_to_all(place(entry_of, by_group, share, pair), 'ctx', split_axis=...]
    ppermute x27 -> x21, starting transfers between devices: 42.6 us -> 37.3 us  [shift(): lax.ppermute(x, 'head', [(i, (i + by) % count) for i in range(count)])]
    pallas_call x5, Pallas kernels: 28.2 us -> 31.9 us  [the longest x1 20.4 us: group_grads(): pl.pallas_call(group_kernel, grid=(groups,), in_specs=[smem(), pl.BlockSp...]
    squeeze x4 -> x0, local copies, waits for them, and re-layouts: 3.65 us -> none  [the longest x3 2.97 us: local(): by_offset[OFFSETS[at][which]] = parts[at * 2 + which][group]]
    convert_element_type x6 -> x10, other arithmetic: 0.43 us -> 3.19 us  [add(): return (a.astype(jnp.float32) + b.astype(jnp.float32)).astype(jnp.bfloat16)]
  transfers between devices with their start and end apart: 29 -> 24, of which waited for: 15 -> 10; matrix products, arithmetic and copies ran while one was open for 9% -> 10% of each run, Pallas kernels for 0% -> 1%
where the time goes in v2:
time: 176 us; the launch traced here: 175 us
  waiting for transfers between devices  58.9 us (33%)
  starting transfers between devices  58 us (33%)
  Pallas kernels  34 us (19%)
  local copies, waits for them, and re-layouts  18 us (10%)
  other arithmetic  4.58 us (3%)
    ppermute x21, starting transfers between devices, shift(): lax.ppermute(x, 'head', [(i, (i + by) % count) for i in range(count)])  37.3 us
    all_to_all x1, waiting for transfers between devices, local(): lax.all_to_all(outgoing, 'ctx', split_axis=0, concat_axis=0, tiled=True)  33.9 us
    pallas_call x1, Pallas kernels, group_grads(): pl.pallas_call(group_kernel, grid=(groups,), in_specs=[smem(), pl.BlockSp...  20.4 us
    ppermute x21, waiting for transfers between devices, shift(): lax.ppermute(x, 'head', [(i, (i + by) % count) for i in range(count)])  15.4 us
    unnamed x50, local copies, waits for them, and re-layouts  13 us
    all_to_all x1, starting transfers between devices, local(): lax.all_to_all(place(entry_of, by_group, share, pair), 'ctx', split_axis=...  7.76 us
    all_to_all x1, starting transfers between devices, local(): lax.all_to_all(spread_rows.reshape(ctx_count, span, 640), 'ctx', split_ax...  7.62 us
    all_to_all x1, waiting for transfers between devices, local(): lax.all_to_all(spread_rows.reshape(ctx_count, span, 640), 'ctx', split_ax...  6.9 us
  transfers between devices with their start and end apart: 24, of which 10 were waited for; matrix products, arithmetic and copies ran while one was open for 10% of the time, Pallas kernels for 1%

profile of v2, /device:TPU:2, one launch (start us, length us, event | category | flops | bytes accessed | tf_op | source)
XLA Modules:
  0.0 174.5 jit_solution(8374655811949285597)
XLA Ops:
  0.6 2.7 %spread.1 = bf16[512,640]{1,0:T(8,128)(2,1)} custom-call(s32[2,16]{1,0:T(2,128)} %lists_ref.3, s32[256]{0:T(256)} %home_ref.3, bf16[576,512]{1,0:T(8,128)(2,1)} %bitcast.87), custom_call_target="tpu_custom_call" | custom-call | tf_op jit(solution)/shard_map/spread/pallas_call | solution.py:87
  3.4 7.6 %all-to-all-start = ((bf16[32,16,640]{2,1,0:T(8,128)(2,1)}), bf16[32,16,640]{2,1,0:T(8,128)(2,1)S(1)}, u32[]{:S(2)}, u32[]{:S(2)}) async-start(bf16[32,16,640]{2,1,0:T(8,128)(2,1)} %bitcast.86), calls=%async_computation | async-start | bytes 1310720 | tf_op jit(solution)/shard_map/all_to_all | solution.py:319
  11.0 1.5 plan.1.index_ref
  12.5 3.5 %copy.10 = bf16[128,16,576]{2,1,0:T(8,128)(2,1)} copy(bf16[128,16,576]{0,2,1:T(8,128)(2,1)S(1)} %copy-done.3) | data formatting | bytes 4718592 | tf_op args[0]
  16.0 6.9 %all-to-all-done = bf16[32,16,640]{2,1,0:T(8,128)(2,1)S(1)} async-done(((bf16[32,16,640]{2,1,0:T(8,128)(2,1)}), bf16[32,16,640]{2,1,0:T(8,128)(2,1)S(1)}, u32[]{:S(2)}, u32[]{:S(2)}) %all-to-all-start) | async-done | bytes 655392 | tf_op jit(solution)/shard_map/all_to_all | solution.py:319
  22.9 0.8 copy-done
  23.7 4.5 %choose.1 = bf16[32,4,16,576]{3,2,1,0:T(8,128)(2,1)} custom-call(bf16[512,640]{1,0:T(8,128)(2,1)} %bitcast.84), custom_call_target="tpu_custom_call" | custom-call | tf_op jit(solution)/shard_map/choose/pallas_call | solution.py:113
  28.2 5.3 %all-to-all-start.1 = ((bf16[32,2,32,576]{3,2,1,0:T(8,128)(2,1)}), bf16[32,2,32,576]{3,2,1,0:T(8,128)(2,1)S(1)}, u32[]{:S(2)}, u32[]{:S(2)}) async-start(bf16[32,2,32,576]{3,2,1,0:T(8,128)(2,1)} %bitcast.81), calls=%async_computation.1 | async-start | bytes 5242880 | tf_op jit(solution)/shard_map/all_to_all | solution.py:329
  33.5 33.9 %all-to-all-done.1.key_ref = bf16[32,2,32,576]{3,2,1,0:T(8,128)(2,1)S(1)} async-done(((bf16[32,2,32,576]{3,2,1,0:T(8,128)(2,1)}), bf16[32,2,32,576]{3,2,1,0:T(8,128)(2,1)S(1)}, u32[]{:S(2)}, u32[]{:S(2)}) %all-to-all-start.1) | async-done | bytes 2359328 | tf_op jit(solution)/shard_map/all_to_all | solution.py:329
  67.4 1.5 copy-done.1
  68.9 20.4 %group_grads.1 = (bf16[2,576,1024]{2,1,0:T(8,128)(2,1)}, f32[128,576]{1,0:T(8,128)}, bf16[128,576]{1,0:T(8,128)(2,1)}, bf16[128,576]{1,0:T(8,128)(2,1)}, bf16[12...) custom-call(s32[1]{0:T(128)} %bitcast.me_ref, ...), custom_call_target="tpu_custom_call" | custom-call | flops 11542724608 | bytes 15000000 | tf_op jit(solution)/shard_map/group_grads/pallas_call | solution.py:245
  89.3 2.0 %collective-permute-start = (bf16[128,576]{1,0:T(8,128)(2,1)}, bf16[128,576]{1,0:T(8,128)(2,1)S(1)}, u32[]{:S(2)}, u32[]{:S(2)}) collective-permute-start(bf16[128,576]{1,0:T(8,128)(2,1)} %get-tuple-element.30), channel_id=1, source_target_pairs={{0,1},{1,2},{2,3},{3,4},{4,5},{5,6},{6,7},{7,0},{8,9},{9,10},{10,1... | collective-permute-start | bytes 442376 | tf_op jit(solution)/shard_map/ppermute | solution.py:267
  91.3 4.2 %collective-permute-start.4 = (bf16[128,576]{1,0:T(8,128)(2,1)}, bf16[128,576]{1,0:T(8,128)(2,1)S(1)}, u32[]{:S(2)}, u32[]{:S(2)}) collective-permute-start(bf16[128,576]{1,0:T(8,128)(2,1)} %get-tuple-element.33), channel_id=1, source_target_pairs={{0,7},{1,0},{2,1},{3,2},{4,3},{5,4},{6,5},{7,6},{8,15},{9,8},{10,9... | collective-permute-start | bytes 442376 | tf_op jit(solution)/shard_map/ppermute | solution.py:267
  95.5 3.2 %collective-permute-start.10 = (bf16[128,576]{1,0:T(8,128)(2,1)}, bf16[128,576]{1,0:T(8,128)(2,1)S(1)}, u32[]{:S(2)}, u32[]{:S(2)}) collective-permute-start(bf16[128,576]{1,0:T(8,128)(2,1)} %get-tuple-element.41), channel_id=1, source_target_pairs={{0,7},{1,0},{2,1},{3,2},{4,3},{5,4},{6,5},{7,6},{8,15},{9,8},{10,9... | collective-permute-start | bytes 442376 | tf_op jit(solution)/shard_map/ppermute | solution.py:267
  98.8 0.7 collective-permute-done
  99.5 1.0 add_convert_fusion.9
  100.6 1.0 add_convert_fusion.6
  101.5 3.3 %collective-permute-start.5 = (bf16[128,576]{1,0:T(8,128)(2,1)S(1)}, bf16[128,576]{1,0:T(8,128)(2,1)S(1)}, u32[]{:S(2)}, u32[]{:S(2)}) collective-permute-start(bf16[128,576]{1,0:T(8,128)(2,1)S(1)} %add_convert_fusion.6), channel_id=1, source_target_pairs={{0,7},{1,0},{2,1},{3,2},{4,3},{5,4},{6,5},{7,6},{8,15},{9,8},{10,9... | collective-permute-start | bytes 442376 | tf_op jit(solution)/shard_map/ppermute | solution.py:267
  104.8 1.0 add_convert_fusion.4
  106.0 3.3 %collective-permute-start.11 = (bf16[128,576]{1,0:T(8,128)(2,1)S(1)}, bf16[128,576]{1,0:T(8,128)(2,1)S(1)}, u32[]{:S(2)}, u32[]{:S(2)}) collective-permute-start(bf16[128,576]{1,0:T(8,128)(2,1)S(1)} %add_convert_fusion.2), channel_id=1, source_target_pairs={{0,7},{1,0},{2,1},{3,2},{4,3},{5,4},{6,5},{7,6},{8,15},{9,8},{10,9... | collective-permute-start | bytes 442376 | tf_op jit(solution)/shard_map/ppermute | solution.py:267
  109.5 3.3 %collective-permute-start.6 = (bf16[128,576]{1,0:T(8,128)(2,1)S(1)}, bf16[128,576]{1,0:T(8,128)(2,1)S(1)}, u32[]{:S(2)}, u32[]{:S(2)}) collective-permute-start(bf16[128,576]{1,0:T(8,128)(2,1)S(1)} %add_convert_fusion.5), channel_id=1, source_target_pairs={{0,7},{1,0},{2,1},{3,2},{4,3},{5,4},{6,5},{7,6},{8,15},{9,8},{10,9... | collective-permute-start | bytes 442376 | tf_op jit(solution)/shard_map/ppermute | solution.py:267
  112.8 1.3 collective-permute-done.8
  114.3 3.3 %collective-permute-start.12 = (bf16[128,576]{1,0:T(8,128)(2,1)S(1)}, bf16[128,576]{1,0:T(8,128)(2,1)S(1)}, u32[]{:S(2)}, u32[]{:S(2)}) collective-permute-start(bf16[128,576]{1,0:T(8,128)(2,1)S(1)} %add_convert_fusion.1), channel_id=1, source_target_pairs={{0,7},{1,0},{2,1},{3,2},{4,3},{5,4},{6,5},{7,6},{8,15},{9,8},{10,9... | collective-permute-start | bytes 442376 | tf_op jit(solution)/shard_map/ppermute | solution.py:267
  117.7 2.9 %collective-permute-done.12 = bf16[128,576]{1,0:T(8,128)(2,1)S(1)} collective-permute-done((bf16[128,576]{1,0:T(8,128)(2,1)S(1)}, bf16[128,576]{1,0:T(8,128)(2,1)S(1)}, u32[]{:S(2)}, u32[]{:S(2)}) %collective-permute-start.12) | collective-permute-done | bytes 147488 | tf_op jit(solution)/shard_map/ppermute | solution.py:267
  120.6 3.8 %collective-permute-start.13 = (bf16[128,576]{1,0:T(8,128)(2,1)S(1)}, bf16[128,576]{1,0:T(8,128)(2,1)S(1)}, u32[]{:S(2)}, u32[]{:S(2)}) collective-permute-start(bf16[128,576]{1,0:T(8,128)(2,1)S(1)} %add_convert_fusion), channel_id=1, source_target_pairs={{0,7},{1,0},{2,1},{3,2},{4,3},{5,4},{6,5},{7,6},{8,15},{9,8},{10,9... | collective-permute-start | bytes 442376 | tf_op jit(solution)/shard_map/ppermute | solution.py:267
  124.4 2.8 %collective-permute-done.13.refs_5_ = bf16[128,576]{1,0:T(8,128)(2,1)S(1)} collective-permute-done((bf16[128,576]{1,0:T(8,128)(2,1)S(1)}, bf16[128,576]{1,0:T(8,128)(2,1)S(1)}, u32[]{:S(2)}, u32[]{:S(2)}) %collective-permute-start.13) | collective-permute-done | bytes 147488 | tf_op jit(solution)/shard_map/ppermute | solution.py:267
  127.2 0.7 copy-done.8
  127.9 2.8 %place.1 = bf16[64,8,576]{2,1,0:T(8,128)(2,1)} custom-call(s32[64]{0:T(128)} %plan.1.index_ref, f32[128,576]{1,0:T(8,128)} %get-tuple-element.26.refs_0_, bf16[128,576]{1,0:T(8,128)(2,1)} %copy-done.7, bf16[128,576]{1,0:T(8,128)(2,1)} %copy-done.5, f32[128,576]{1,0:T(8,128)} %get-tuple-element.34.refs_3_, bf16[128,576]{1,0:T(8,128)(2,1)} %copy-done.6, ...), custom_call_target="tpu_custom_call" | custom-call | tf_op jit(solution)/shard_map/place/pallas_call | solution.py:153
  130.7 7.8 %all-to-all-start.2 = ((bf16[64,8,576]{2,1,0:T(8,128)(2,1)}), bf16[64,8,576]{2,1,0:T(8,128)(2,1)S(1)}, u32[]{:S(2)}, u32[]{:S(2)}) async-start(bf16[64,8,576]{2,1,0:T(8,128)(2,1)} %place.1), calls=%async_computation.2 | async-start | bytes 1310720 | tf_op jit(solution)/shard_map/all_to_all | solution.py:344
  138.5 1.1 slice.3
  139.6 1.3 select_reduce_fusion.1
  140.9 0.1 copy.12
  141.0 0.6 reshape.146.index_ref
  141.6 3.1 %copy.11 = bf16[2,576,1024]{1,2,0:T(8,128)(2,1)S(1)} copy(bf16[2,576,1024]{2,1,0:T(8,128)(2,1)} %get-tuple-element.24) | data formatting | bytes 4718592 | tf_op jit(solution)/shard_map/group_grads/pallas_call | solution.py:245
  144.7 3.1 %copy.14 = bf16[128,16,576]{0,2,1:T(8,128)(2,1)} copy(bf16[128,16,576]{2,1,0:T(8,128)(2,1)S(1)} %bitcast.82) | data formatting | bytes 4718592
  147.8 2.7 %all-to-all-done.2.rows_ref = bf16[64,8,576]{2,1,0:T(8,128)(2,1)S(1)} async-done(((bf16[64,8,576]{2,1,0:T(8,128)(2,1)}), bf16[64,8,576]{2,1,0:T(8,128)(2,1)S(1)}, u32[]{:S(2)}, u32[]{:S(2)}) %all-to-all-start.2) | async-done | bytes 589856 | tf_op jit(solution)/shard_map/all_to_all | solution.py:344
  150.5 0.8 copy-done.2
  151.3 2.1 %gather_sum.1 = bf16[8,8,576]{2,1,0:T(8,128)(2,1)} custom-call(s32[64]{0:T(128)} %reshape.146.index_ref, bf16[64,8,576]{2,1,0:T(8,128)(2,1)} %copy-done.2), custom_call_target="tpu_custom_call" | custom-call | tf_op jit(solution)/shard_map/gather_sum/pallas_call | solution.py:177
  153.4 5.5 %collective-permute-start.17 = (bf16[8,8,576]{2,1,0:T(8,128)(2,1)}, bf16[8,8,576]{2,1,0:T(8,128)(2,1)S(1)}, u32[]{:S(2)}, u32[]{:S(2)}) collective-permute-start(bf16[8,8,576]{2,1,0:T(8,128)(2,1)} %gather_sum.1), channel_id=1, source_target_pairs={{0,2},{1,3},{2,4},{3,5},{4,6},{5,7},{6,0},{7,1},{8,10},{9,11},{10,... | collective-permute-start | bytes 221192 | tf_op jit(solution)/shard_map/ppermute | solution.py:267
  158.9 1.1 collective-permute-start.14
  160.0 0.9 bitcast_dynamic-update-slice_fusion.14
  161.0 4.3 %collective-permute-done.17 = bf16[8,8,576]{2,1,0:T(8,128)(2,1)S(1)} collective-permute-done((bf16[8,8,576]{2,1,0:T(8,128)(2,1)}, bf16[8,8,576]{2,1,0:T(8,128)(2,1)S(1)}, u32[]{:S(2)}, u32[]{:S(2)}) %collective-permute-start.17) | collective-permute-done | bytes 73760 | tf_op jit(solution)/shard_map/ppermute | solution.py:267
  165.3 0.7 collective-permute-start.18
  166.0 3.2 %collective-permute-start.16 = (bf16[8,8,576]{2,1,0:T(8,128)(2,1)S(1)}, bf16[8,8,576]{2,1,0:T(8,128)(2,1)S(1)}, u32[]{:S(2)}, u32[]{:S(2)}) collective-permute-start(bf16[8,8,576]{2,1,0:T(8,128)(2,1)S(1)} %collective-permute-done.15), channel_id=1, source_target_pairs={{0,7},{1,0},{2,1},{3,2},{4,3},{5,4},{6,5},{7,6},{8,15},{9,8},{10,9... | collective-permute-start | bytes 221192 | tf_op jit(solution)/shard_map/ppermute | solution.py:267
  169.3 3.1 %collective-permute-done.16 = bf16[8,8,576]{2,1,0:T(8,128)(2,1)S(1)} collective-permute-done((bf16[8,8,576]{2,1,0:T(8,128)(2,1)S(1)}, bf16[8,8,576]{2,1,0:T(8,128)(2,1)S(1)}, u32[]{:S(2)}, u32[]{:S(2)}) %collective-permute-start.16) | collective-permute-done | bytes 73760 | tf_op jit(solution)/shard_map/ppermute | solution.py:267
  172.5 0.2 collective-permute-done.19
  172.9 0.1 convert_bitcast_fusion
  173.1 1.4 copy.15
  (77 shorter events, 1.2 us)
Async XLA Ops:
  0.6 11.9 %copy-start.3 = (bf16[128,16,576]{0,2,1:T(8,128)(2,1)S(1)}, bf16[128,16,576]{0,2,1:T(8,128)(2,1)}, u32[]{:S(2)}) copy-start(bf16[128,16,576]{0,2,1:T(8,128)(2,1)} %param.5) | copy-start | bytes 7077892
  3.4 19.5 %all-to-all-start = ((bf16[32,16,640]{2,1,0:T(8,128)(2,1)}), bf16[32,16,640]{2,1,0:T(8,128)(2,1)S(1)}, u32[]{:S(2)}, u32[]{:S(2)}) async-start(bf16[32,16,640]{2,1,0:T(8,128)(2,1)} %bitcast.86), calls=%async_computation | async-start | bytes 1310720 | tf_op jit(solution)/shard_map/all_to_all | solution.py:319
  22.9 0.8 copy-start
  28.2 39.2 %all-to-all-start.1 = ((bf16[32,2,32,576]{3,2,1,0:T(8,128)(2,1)}), bf16[32,2,32,576]{3,2,1,0:T(8,128)(2,1)S(1)}, u32[]{:S(2)}, u32[]{:S(2)}) async-start(bf16[32,2,32,576]{3,2,1,0:T(8,128)(2,1)} %bitcast.81), calls=%async_computation.1 | async-start | bytes 5242880 | tf_op jit(solution)/shard_map/all_to_all | solution.py:329
  67.4 1.5 copy-start.1
  89.3 16.6 %copy-start.15 = (bf16[128,576]{1,0:T(8,128)(2,1)S(1)}, bf16[128,576]{1,0:T(8,128)(2,1)}, u32[]{:S(2)}) copy-start(bf16[128,576]{1,0:T(8,128)(2,1)} %get-tuple-element.40) | copy-start | bytes 442372
  89.3 19.9 %copy-start.14 = (bf16[128,576]{1,0:T(8,128)(2,1)S(1)}, bf16[128,576]{1,0:T(8,128)(2,1)}, u32[]{:S(2)}) copy-start(bf16[128,576]{1,0:T(8,128)(2,1)} %get-tuple-element.28) | copy-start | bytes 442372
  89.3 20.1 %copy-start.13 = (bf16[128,576]{1,0:T(8,128)(2,1)S(1)}, bf16[128,576]{1,0:T(8,128)(2,1)}, u32[]{:S(2)}) copy-start(bf16[128,576]{1,0:T(8,128)(2,1)} %get-tuple-element.31) | copy-start | bytes 442372
  89.3 10.1 %collective-permute-start = (bf16[128,576]{1,0:T(8,128)(2,1)}, bf16[128,576]{1,0:T(8,128)(2,1)S(1)}, u32[]{:S(2)}, u32[]{:S(2)}) collective-permute-start(bf16[128,576]{1,0:T(8,128)(2,1)} %get-tuple-element.30), channel_id=1, source_target_pairs={{0,1},{1,2},{2,3},{3,4},{4,5},{5,6},{6,7},{7,0},{8,9},{9,10},{10,1... | collective-permute-start | bytes 442376 | tf_op jit(solution)/shard_map/ppermute | solution.py:267
  91.3 9.2 %collective-permute-start.4 = (bf16[128,576]{1,0:T(8,128)(2,1)}, bf16[128,576]{1,0:T(8,128)(2,1)S(1)}, u32[]{:S(2)}, u32[]{:S(2)}) collective-permute-start(bf16[128,576]{1,0:T(8,128)(2,1)} %get-tuple-element.33), channel_id=1, source_target_pairs={{0,7},{1,0},{2,1},{3,2},{4,3},{5,4},{6,5},{7,6},{8,15},{9,8},{10,9... | collective-permute-start | bytes 442376 | tf_op jit(solution)/shard_map/ppermute | solution.py:267
  95.5 9.3 %collective-permute-start.7 = (bf16[128,576]{1,0:T(8,128)(2,1)}, bf16[128,576]{1,0:T(8,128)(2,1)S(1)}, u32[]{:S(2)}, u32[]{:S(2)}) collective-permute-start(bf16[128,576]{1,0:T(8,128)(2,1)} %get-tuple-element.37), channel_id=1, source_target_pairs={{0,1},{1,2},{2,3},{3,4},{4,5},{5,6},{6,7},{7,0},{8,9},{9,10},{10,1... | collective-permute-start | bytes 442376 | tf_op jit(solution)/shard_map/ppermute | solution.py:267
  95.5 10.4 %collective-permute-start.10 = (bf16[128,576]{1,0:T(8,128)(2,1)}, bf16[128,576]{1,0:T(8,128)(2,1)S(1)}, u32[]{:S(2)}, u32[]{:S(2)}) collective-permute-start(bf16[128,576]{1,0:T(8,128)(2,1)} %get-tuple-element.41), channel_id=1, source_target_pairs={{0,7},{1,0},{2,1},{3,2},{4,3},{5,4},{6,5},{7,6},{8,15},{9,8},{10,9... | collective-permute-start | bytes 442376 | tf_op jit(solution)/shard_map/ppermute | solution.py:267
  100.4 13.6 %copy-start.12 = (bf16[128,576]{1,0:T(8,128)(2,1)S(1)}, bf16[128,576]{1,0:T(8,128)(2,1)}, u32[]{:S(2)}) copy-start(bf16[128,576]{1,0:T(8,128)(2,1)} %get-tuple-element.35) | copy-start | bytes 442372
  100.5 8.8 %collective-permute-start.1 = (bf16[128,576]{1,0:T(8,128)(2,1)S(1)}, bf16[128,576]{1,0:T(8,128)(2,1)S(1)}, u32[]{:S(2)}, u32[]{:S(2)}) collective-permute-start(bf16[128,576]{1,0:T(8,128)(2,1)S(1)} %add_convert_fusion.9), channel_id=1, source_target_pairs={{0,1},{1,2},{2,3},{3,4},{4,5},{5,6},{6,7},{7,0},{8,9},{9,10},{10,1... | collective-permute-start | bytes 442376 | tf_op jit(solution)/shard_map/ppermute | solution.py:267
  101.5 12.7 %copy-start.11 = (bf16[128,576]{1,0:T(8,128)(2,1)S(1)}, bf16[128,576]{1,0:T(8,128)(2,1)}, u32[]{:S(2)}) copy-start(bf16[128,576]{1,0:T(8,128)(2,1)} %get-tuple-element.39) | copy-start | bytes 442372
  101.5 7.9 %collective-permute-start.5 = (bf16[128,576]{1,0:T(8,128)(2,1)S(1)}, bf16[128,576]{1,0:T(8,128)(2,1)S(1)}, u32[]{:S(2)}, u32[]{:S(2)}) collective-permute-start(bf16[128,576]{1,0:T(8,128)(2,1)S(1)} %add_convert_fusion.6), channel_id=1, source_target_pairs={{0,7},{1,0},{2,1},{3,2},{4,3},{5,4},{6,5},{7,6},{8,15},{9,8},{10,9... | collective-permute-start | bytes 442376 | tf_op jit(solution)/shard_map/ppermute | solution.py:267
  105.8 11.7 %copy-start.10 = (bf16[128,576]{1,0:T(8,128)(2,1)S(1)}, bf16[128,576]{1,0:T(8,128)(2,1)}, u32[]{:S(2)}) copy-start(bf16[128,576]{1,0:T(8,128)(2,1)} %get-tuple-element.27) | copy-start | bytes 442372
  105.8 8.2 %collective-permute-start.8 = (bf16[128,576]{1,0:T(8,128)(2,1)S(1)}, bf16[128,576]{1,0:T(8,128)(2,1)S(1)}, u32[]{:S(2)}, u32[]{:S(2)}) collective-permute-start(bf16[128,576]{1,0:T(8,128)(2,1)S(1)} %add_convert_fusion.4), channel_id=1, source_target_pairs={{0,1},{1,2},{2,3},{3,4},{4,5},{5,6},{6,7},{7,0},{8,9},{9,10},{10,1... | collective-permute-start | bytes 442376 | tf_op jit(solution)/shard_map/ppermute | solution.py:267
  106.0 14.6 %copy-start.9 = (bf16[128,576]{1,0:T(8,128)(2,1)S(1)}, bf16[128,576]{1,0:T(8,128)(2,1)}, u32[]{:S(2)}) copy-start(bf16[128,576]{1,0:T(8,128)(2,1)} %get-tuple-element.38) | copy-start | bytes 442372
  106.0 8.2 %collective-permute-start.11 = (bf16[128,576]{1,0:T(8,128)(2,1)S(1)}, bf16[128,576]{1,0:T(8,128)(2,1)S(1)}, u32[]{:S(2)}, u32[]{:S(2)}) collective-permute-start(bf16[128,576]{1,0:T(8,128)(2,1)S(1)} %add_convert_fusion.2), channel_id=1, source_target_pairs={{0,7},{1,0},{2,1},{3,2},{4,3},{5,4},{6,5},{7,6},{8,15},{9,8},{10,9... | collective-permute-start | bytes 442376 | tf_op jit(solution)/shard_map/ppermute | solution.py:267
  109.3 8.2 %collective-permute-start.2 = (bf16[128,576]{1,0:T(8,128)(2,1)S(1)}, bf16[128,576]{1,0:T(8,128)(2,1)S(1)}, u32[]{:S(2)}, u32[]{:S(2)}) collective-permute-start(bf16[128,576]{1,0:T(8,128)(2,1)S(1)} %add_convert_fusion.8), channel_id=1, source_target_pairs={{0,1},{1,2},{2,3},{3,4},{4,5},{5,6},{6,7},{7,0},{8,9},{9,10},{10,1... | collective-permute-start | bytes 442376 | tf_op jit(solution)/shard_map/ppermute | solution.py:267
  109.5 14.9 %collective-permute-start.6 = (bf16[128,576]{1,0:T(8,128)(2,1)S(1)}, bf16[128,576]{1,0:T(8,128)(2,1)S(1)}, u32[]{:S(2)}, u32[]{:S(2)}) collective-permute-start(bf16[128,576]{1,0:T(8,128)(2,1)S(1)} %add_convert_fusion.5), channel_id=1, source_target_pairs={{0,7},{1,0},{2,1},{3,2},{4,3},{5,4},{6,5},{7,6},{8,15},{9,8},{10,9... | collective-permute-start | bytes 442376 | tf_op jit(solution)/shard_map/ppermute | solution.py:267
  114.1 10.3 %collective-permute-start.9 = (bf16[128,576]{1,0:T(8,128)(2,1)S(1)}, bf16[128,576]{1,0:T(8,128)(2,1)S(1)}, u32[]{:S(2)}, u32[]{:S(2)}) collective-permute-start(bf16[128,576]{1,0:T(8,128)(2,1)S(1)} %add_convert_fusion.3), channel_id=1, source_target_pairs={{0,1},{1,2},{2,3},{3,4},{4,5},{5,6},{6,7},{7,0},{8,9},{9,10},{10,1... | collective-permute-start | bytes 442376 | tf_op jit(solution)/shard_map/ppermute | solution.py:267
  114.3 6.3 %collective-permute-start.12 = (bf16[128,576]{1,0:T(8,128)(2,1)S(1)}, bf16[128,576]{1,0:T(8,128)(2,1)S(1)}, u32[]{:S(2)}, u32[]{:S(2)}) collective-permute-start(bf16[128,576]{1,0:T(8,128)(2,1)S(1)} %add_convert_fusion.1), channel_id=1, source_target_pairs={{0,7},{1,0},{2,1},{3,2},{4,3},{5,4},{6,5},{7,6},{8,15},{9,8},{10,9... | collective-permute-start | bytes 442376 | tf_op jit(solution)/shard_map/ppermute | solution.py:267
  117.6 6.8 %collective-permute-start.3 = (bf16[128,576]{1,0:T(8,128)(2,1)S(1)}, bf16[128,576]{1,0:T(8,128)(2,1)S(1)}, u32[]{:S(2)}, u32[]{:S(2)}) collective-permute-start(bf16[128,576]{1,0:T(8,128)(2,1)S(1)} %add_convert_fusion.7), channel_id=1, source_target_pairs={{0,1},{1,2},{2,3},{3,4},{4,5},{5,6},{6,7},{7,0},{8,9},{9,10},{10,1... | collective-permute-start | bytes 442376 | tf_op jit(solution)/shard_map/ppermute | solution.py:267
  120.6 6.6 %collective-permute-start.13 = (bf16[128,576]{1,0:T(8,128)(2,1)S(1)}, bf16[128,576]{1,0:T(8,128)(2,1)S(1)}, u32[]{:S(2)}, u32[]{:S(2)}) collective-permute-start(bf16[128,576]{1,0:T(8,128)(2,1)S(1)} %add_convert_fusion), channel_id=1, source_target_pairs={{0,7},{1,0},{2,1},{3,2},{4,3},{5,4},{6,5},{7,6},{8,15},{9,8},{10,9... | collective-permute-start | bytes 442376 | tf_op jit(solution)/shard_map/ppermute | solution.py:267
  124.4 2.8 %copy-start.5 = (bf16[128,576]{1,0:T(8,128)(2,1)}, bf16[128,576]{1,0:T(8,128)(2,1)S(1)}, u32[]{:S(2)}) copy-start(bf16[128,576]{1,0:T(8,128)(2,1)S(1)} %collective-permute-done.6.refs_2_) | copy-start | bytes 442372
  124.4 2.8 %copy-start.6 = (bf16[128,576]{1,0:T(8,128)(2,1)}, bf16[128,576]{1,0:T(8,128)(2,1)S(1)}, u32[]{:S(2)}) copy-start(bf16[128,576]{1,0:T(8,128)(2,1)S(1)} %collective-permute-done.9.refs_4_) | copy-start | bytes 442372
  124.4 2.8 %copy-start.7 = (bf16[128,576]{1,0:T(8,128)(2,1)}, bf16[128,576]{1,0:T(8,128)(2,1)S(1)}, u32[]{:S(2)}) copy-start(bf16[128,576]{1,0:T(8,128)(2,1)S(1)} %collective-permute-done.3.refs_1_) | copy-start | bytes 442372
  127.2 0.7 copy-start.8
  130.7 19.8 %all-to-all-start.2 = ((bf16[64,8,576]{2,1,0:T(8,128)(2,1)}), bf16[64,8,576]{2,1,0:T(8,128)(2,1)S(1)}, u32[]{:S(2)}, u32[]{:S(2)}) async-start(bf16[64,8,576]{2,1,0:T(8,128)(2,1)} %place.1), calls=%async_computation.2 | async-start | bytes 1310720 | tf_op jit(solution)/shard_map/all_to_all | solution.py:344
  150.5 0.8 copy-start.2
  153.4 19.3 %copy-start.4 = (bf16[8,8,576]{2,1,0:T(8,128)(2,1)S(1)}, bf16[8,8,576]{2,1,0:T(8,128)(2,1)}, u32[]{:S(2)}) copy-start(bf16[8,8,576]{2,1,0:T(8,128)(2,1)} %gather_sum.1) | copy-start | bytes 221188
  153.4 19.3 %collective-permute-start.20 = (bf16[8,8,576]{2,1,0:T(8,128)(2,1)}, bf16[8,8,576]{2,1,0:T(8,128)(2,1)S(1)}, u32[]{:S(2)}, u32[]{:S(2)}) collective-permute-start(bf16[8,8,576]{2,1,0:T(8,128)(2,1)} %gather_sum.1), channel_id=1, source_target_pairs={{0,1},{1,2},{2,3},{3,4},{4,5},{5,6},{6,7},{7,0},{8,9},{9,10},{10,1... | collective-permute-start | bytes 221192 | tf_op jit(solution)/shard_map/ppermute | solution.py:267
  153.4 11.9 %collective-permute-start.17 = (bf16[8,8,576]{2,1,0:T(8,128)(2,1)}, bf16[8,8,576]{2,1,0:T(8,128)(2,1)S(1)}, u32[]{:S(2)}, u32[]{:S(2)}) collective-permute-start(bf16[8,8,576]{2,1,0:T(8,128)(2,1)} %gather_sum.1), channel_id=1, source_target_pairs={{0,2},{1,3},{2,4},{3,5},{4,6},{5,7},{6,0},{7,1},{8,10},{9,11},{10,... | collective-permute-start | bytes 221192 | tf_op jit(solution)/shard_map/ppermute | solution.py:267
  158.9 7.1 %collective-permute-start.15 = (bf16[8,8,576]{2,1,0:T(8,128)(2,1)}, bf16[8,8,576]{2,1,0:T(8,128)(2,1)S(1)}, u32[]{:S(2)}, u32[]{:S(2)}) collective-permute-start(bf16[8,8,576]{2,1,0:T(8,128)(2,1)} %gather_sum.1), channel_id=1, source_target_pairs={{0,6},{1,7},{2,0},{3,1},{4,2},{5,3},{6,4},{7,5},{8,14},{9,15},{10,... | collective-permute-start | bytes 221192 | tf_op jit(solution)/shard_map/ppermute | solution.py:267
  158.9 10.4 %collective-permute-start.14 = (bf16[8,8,576]{2,1,0:T(8,128)(2,1)}, bf16[8,8,576]{2,1,0:T(8,128)(2,1)S(1)}, u32[]{:S(2)}, u32[]{:S(2)}) collective-permute-start(bf16[8,8,576]{2,1,0:T(8,128)(2,1)} %gather_sum.1), channel_id=1, source_target_pairs={{0,7},{1,0},{2,1},{3,2},{4,3},{5,4},{6,5},{7,6},{8,15},{9,8},{10,9... | collective-permute-start | bytes 221192 | tf_op jit(solution)/shard_map/ppermute | solution.py:267
  165.3 7.4 %collective-permute-start.19 = (bf16[8,8,576]{2,1,0:T(8,128)(2,1)S(1)}, bf16[8,8,576]{2,1,0:T(8,128)(2,1)S(1)}, u32[]{:S(2)}, u32[]{:S(2)}) collective-permute-start(bf16[8,8,576]{2,1,0:T(8,128)(2,1)S(1)} %collective-permute-done.17), channel_id=1, source_target_pairs={{0,1},{1,2},{2,3},{3,4},{4,5},{5,6},{6,7},{7,0},{8,9},{9,10},{10,1... | collective-permute-start | bytes 221192 | tf_op jit(solution)/shard_map/ppermute | solution.py:267
  165.3 7.1 %collective-permute-start.18 = (bf16[8,8,576]{2,1,0:T(8,128)(2,1)S(1)}, bf16[8,8,576]{2,1,0:T(8,128)(2,1)S(1)}, u32[]{:S(2)}, u32[]{:S(2)}) collective-permute-start(bf16[8,8,576]{2,1,0:T(8,128)(2,1)S(1)} %collective-permute-done.17), channel_id=1, source_target_pairs={{0,2},{1,3},{2,4},{3,5},{4,6},{5,7},{6,0},{7,1},{8,10},{9,11},{10,... | collective-permute-start | bytes 221192 | tf_op jit(solution)/shard_map/ppermute | solution.py:267
  166.0 6.4 %collective-permute-start.16 = (bf16[8,8,576]{2,1,0:T(8,128)(2,1)S(1)}, bf16[8,8,576]{2,1,0:T(8,128)(2,1)S(1)}, u32[]{:S(2)}, u32[]{:S(2)}) collective-permute-start(bf16[8,8,576]{2,1,0:T(8,128)(2,1)S(1)} %collective-permute-done.15), channel_id=1, source_target_pairs={{0,7},{1,0},{2,1},{3,2},{4,3},{5,4},{6,5},{7,6},{8,15},{9,8},{10,9... | collective-permute-start | bytes 221192 | tf_op jit(solution)/shard_map/ppermute | solution.py:267
